TPU v7x, 128 devices: a whole 4x4x4 slice. The times are simulated.
128 devices in a mesh: aa: 4 (over z), ba: 16 (over x, y), ma: 2 (over core).
Axes of the slice: x: 4, y: 4, z: 4, core: 2. Of those that a mesh axis runs over, the one named last changes fastest.
Arguments:
- docs: bfloat16 [1024, 16, 1024], P(('aa', 'ba')), may hold values from -6 to 6
- cot: bfloat16 [1024, 16, 1024], P(('aa', 'ba')), may hold values from -6 to 6
- route: int32 [1024, 1], P(('aa', 'ba')), may hold values from 0 to 15; in each aligned block of 16 rows (0 to 15, 16 to 31, ...) at most 2 rows name the same one
- doc_len: int32 [1024], P(('aa', 'ba')), may hold values from 1 to 16
- wt1: float32 [4, 2, 1024, 4096], P('aa', None, 'ba', 'ma'), may hold values from -0.1875 to 0.1875
- mom1: float32 [4, 2, 1024, 4096], P('aa', None, 'ba', 'ma'), may hold values from -6 to 6
- wt2: float32 [16, 2, 1024, 4096], P('ba', None, 'aa', 'ma'), may hold values from -0.1875 to 0.1875
- mom2: float32 [16, 2, 1024, 4096], P('ba', None, 'aa', 'ma'), may hold values from -6 to 6
Outputs:
- new_wt1: float32 [4, 2, 1024, 4096], P('aa', None, 'ba', 'ma')
- new_mom1: float32 [4, 2, 1024, 4096], P('aa', None, 'ba', 'ma')
- new_wt2: float32 [16, 2, 1024, 4096], P('ba', None, 'aa', 'ma')
- new_mom2: float32 [16, 2, 1024, 4096], P('ba', None, 'aa', 'ma')
Inputs may be any that keep to these rules, and one draw needn't show every extreme that they name: `route`: among the 16 documents of one group, no level-2 module is named more than 2 times.
All inputs are finite; a program needn't handle non-finite values.
Results may differ from a plain program's by a relative error of at most 0.023.
Values may be sent and summed in bfloat16 or wider, within the bound.
A program may use at most 256 MiB of HBM per device.

v0:
```python
import jax
import jax.numpy as jnp
from jax import lax
from jax.sharding import PartitionSpec as P

SLOT = 2


EPS = 1e-05
MOMENTUM = 0.9
OUTER_RATE = 0.7


def normalize(inputs):
    floated = inputs.astype(jnp.float32)
    factor = lax.rsqrt(jnp.mean(floated * floated, axis=-1, keepdims=True) + EPS)
    normed = floated * factor
    return (floated, factor, normed, normed.astype(jnp.bfloat16))


def join_halves(partial_value):
    return lax.psum(partial_value.astype(jnp.bfloat16), "ma").astype(jnp.float32)


def slopes_of(upstream, preact, weights):
    incoming = jnp.dot(upstream, weights[1], preferred_element_type=jnp.float32)
    sigma = jax.nn.sigmoid(preact)
    return (incoming * sigma * (1.0 + preact * (1.0 - sigma))).astype(jnp.bfloat16)


def weight_terms(normed_low, slopes, upstream, active):
    first = lax.dot_general(
        normed_low, slopes, (((0,), (0,)), ((), ())), preferred_element_type=jnp.float32
    )
    second = lax.dot_general(
        upstream, active, (((0,), (0,)), ((), ())), preferred_element_type=jnp.float32
    )
    return jnp.stack([first, second])


def outer_step(weights, moment, delta):
    new_moment = MOMENTUM * moment + delta[None]
    return (weights - OUTER_RATE * (delta[None] + MOMENTUM * new_moment), new_moment)


def local(docs, cot, route, doc_len, wt1, mom1, wt2, mom2):
    blocks, block, width = docs.shape
    groups = lax.axis_size("ba")
    levels = lax.axis_size("aa")
    slots = groups * SLOT
    inside = lax.broadcasted_iota(jnp.int32, (blocks, block), 1) < doc_len[:, None]
    masked = jnp.where(inside[:, :, None], cot, jnp.zeros_like(cot))
    targets = route[:, 0]
    shared = targets[:, None] == targets[None, :]
    before = lax.broadcasted_iota(jnp.int32, (blocks, blocks), 0) > lax.broadcasted_iota(
        jnp.int32, (blocks, blocks), 1
    )
    rank = jnp.sum((shared & before).astype(jnp.int32), axis=1)
    target_slot = targets * SLOT + rank
    selector = (lax.broadcasted_iota(jnp.int32, (slots, blocks), 0) == target_slot[None, :]).astype(
        jnp.bfloat16
    )

    def to_slots(values):
        packed = jnp.einsum("sp,ptc->stc", selector, values, preferred_element_type=jnp.float32)
        return packed.astype(jnp.bfloat16).reshape(groups, SLOT * block, width)

    weights_one = lax.all_gather(wt1.astype(jnp.bfloat16), "ba", axis=2, tiled=True)[0]
    floated, factor, normed, normed_low = normalize(docs.reshape(-1, width))
    preact = jnp.dot(normed_low, weights_one[0], preferred_element_type=jnp.float32)
    active = jax.nn.silu(preact).astype(jnp.bfloat16)
    partial_value = lax.dot_general(
        active, weights_one[1], (((1,), (1,)), ((), ())), preferred_element_type=jnp.float32
    )
    output = (floated + join_halves(partial_value)).astype(jnp.bfloat16)
    moved_rows, moved_cot = (
        lax.all_to_all(
            to_slots(output.reshape(blocks, block, width)),
            "ba",
            split_axis=0,
            concat_axis=0,
            tiled=True,
        ),
        lax.all_to_all(to_slots(masked), "ba", split_axis=0, concat_axis=0, tiled=True),
    )
    inputs_two = moved_rows.reshape(-1, width)
    weights_two = lax.all_gather(wt2.astype(jnp.bfloat16), "aa", axis=2, tiled=True)[0]
    upstream_two = moved_cot.reshape(-1, width)
    floated_two, factor_two, normed_two, normed_low_two = normalize(inputs_two)
    preact_two = jnp.dot(normed_low_two, weights_two[0], preferred_element_type=jnp.float32)
    active_two = jax.nn.silu(preact_two).astype(jnp.bfloat16)
    slopes_two = slopes_of(upstream_two, preact_two, weights_two)
    terms_two = weight_terms(normed_low_two, slopes_two, upstream_two, active_two)
    partial_back = lax.dot_general(
        slopes_two, weights_two[0], (((1,), (1,)), ((), ())), preferred_element_type=jnp.float32
    )
    dnorm = join_halves(partial_back)
    back_two = upstream_two.astype(jnp.float32) + factor_two * (
        dnorm - normed_two * jnp.mean(dnorm * normed_two, axis=-1, keepdims=True)
    )
    back_two = back_two.astype(jnp.bfloat16)
    returned = lax.all_to_all(
        back_two.reshape(groups, SLOT * block, width), "ba", split_axis=0, concat_axis=0, tiled=True
    )
    upstream_one = jnp.einsum(
        "sp,stc->ptc",
        selector,
        returned.reshape(slots, block, width),
        preferred_element_type=jnp.float32,
    )
    upstream_one = upstream_one.astype(jnp.bfloat16).reshape(-1, width)
    slopes_one = slopes_of(upstream_one, preact, weights_one)
    terms_one = weight_terms(normed_low, slopes_one, upstream_one, active)
    summed_one = lax.psum_scatter(
        terms_one.astype(jnp.bfloat16), "ba", scatter_dimension=1, tiled=True
    ).astype(jnp.float32)
    summed_two = lax.psum_scatter(
        terms_two.astype(jnp.bfloat16), "aa", scatter_dimension=1, tiled=True
    ).astype(jnp.float32)
    new_wt1, new_mom1 = outer_step(wt1, mom1, summed_one / groups)
    new_wt2, new_mom2 = outer_step(wt2, mom2, summed_two / levels)
    return (new_wt1, new_mom1, new_wt2, new_mom2)


def solution(mesh):
    return jax.shard_map(
        local,
        mesh=mesh,
        in_specs=(
            P(("aa", "ba"), None, None),
            P(("aa", "ba"), None, None),
            P(("aa", "ba"), None),
            P(("aa", "ba")),
            P("aa", None, "ba", "ma"),
            P("aa", None, "ba", "ma"),
            P("ba", None, "aa", "ma"),
            P("ba", None, "aa", "ma"),
        ),
        out_specs=(
            P("aa", None, "ba", "ma"),
            P("aa", None, "ba", "ma"),
            P("ba", None, "aa", "ma"),
            P("ba", None, "aa", "ma"),
        ),
        check_vma=False,
    )
```

profile of v0, /device:TPU:1, one launch (start us, length us, event | category | flops | bytes accessed | tf_op | source)
XLA Modules:
  0.0 419.3 jit_solution(9422900322819601062)
XLA Ops:
  8.0 0.0 all-gather.3.cloned.1.call-start
  8.0 2.1 convert_element_type.105
  10.1 0.0 all-gather.3.cloned.1.call-update
  10.2 0.0 all-reduce.3.cloned.1.call-start
  10.2 1.2 fusion.21
  11.4 1.2 fusion.22
  12.6 72.8 %all-gather.3.cloned.1.call-done = bf16[1,2,1024,2048]{3,2,1,0:T(8,128)(2,1)} async-done(((bf16[1,2,64,2048]{3,2,1,0:T(8,128)(2,1)}), bf16[1,2,1024,2048]{3,2,1,0:T(8,128)(2,1)}) %all-gather.3.cloned.1.call-update) | async-done | bytes 8388624 | tf_op jit(solution)/shard_map/all_gather | solution.py:68
  85.5 3.4 fusion.1
  88.9 1.3 copy-done.9
  90.2 4.3 %fusion.18 = bf16[256,1024]{1,0:T(8,128)(2,1)} fusion(bf16[1,2,1024,2048]{3,2,1,0:T(8,128)(2,1)} %all-gather.3.cloned.1.call-done, f32[256,2048]{1,0:T(8,128)S(1)} %fusion.1), kind=kOutput, calls=%fused_computation.43 | convolution fusion | flops 1076625408 | bytes 6815744 | tf_op jit(solution)/shard_map/dot_general | solution.py:72
  94.5 0.0 all-reduce.3.cloned.1.call-update
  94.5 0.0 copy-start.8
  94.5 0.0 copy-start
  94.6 0.0 all-gather.5.cloned.1.call-start
  94.6 3.9 convert_element_type.112
  98.5 0.0 all-gather.5.cloned.1.call-update
  98.5 0.0 copy-start.6
  98.5 0.0 copy-start.4
  98.5 0.1 rsqrt.25
  98.6 0.2 convert_reduce_fusion
  98.8 20.3 %all-reduce.3.cloned.1.call-done = bf16[256,1024]{1,0:T(8,128)(2,1)} async-done(((bf16[256,1024]{1,0:T(8,128)(2,1)}), bf16[256,1024]{1,0:T(8,128)(2,1)}) %all-reduce.3.cloned.1.call-update) | async-done | bytes 524304 | tf_op jit(solution)/shard_map/psum | solution.py:22
  119.1 2.1 fusion.23
  121.2 0.6 convolution_convert_fusion
  121.8 1.5 copy.23
  123.3 6.6 %all-to-all-start.1 = ((bf16[16,32,1024]{2,1,0:T(8,128)(2,1)}), bf16[16,32,1024]{2,1,0:T(8,128)(2,1)S(1)}, u32[]{:S(2)}, u32[]{:S(2)}) async-start(bf16[16,32,1024]{2,1,0:T(8,128)(2,1)} %bitcast.9), calls=%async_computation.1 | async-start | bytes 2097152 | tf_op jit(solution)/shard_map/all_to_all | solution.py:77
  130.0 0.1 iota_compare_fusion
  130.0 0.1 broadcast_select_fusion
  130.2 0.6 convolution_convert_fusion.1
  130.7 1.5 copy.21
  132.3 13.5 %all-to-all-done.1 = bf16[16,32,1024]{2,1,0:T(8,128)(2,1)S(1)} async-done(((bf16[16,32,1024]{2,1,0:T(8,128)(2,1)}), bf16[16,32,1024]{2,1,0:T(8,128)(2,1)S(1)}, u32[]{:S(2)}, u32[]{:S(2)}) %all-to-all-start.1) | async-done | bytes 1048608 | tf_op jit(solution)/shard_map/all_to_all | solution.py:77
  145.8 4.5 %all-to-all-start = ((bf16[16,32,1024]{2,1,0:T(8,128)(2,1)}), bf16[16,32,1024]{2,1,0:T(8,128)(2,1)S(1)}, u32[]{:S(2)}, u32[]{:S(2)}) async-start(bf16[16,32,1024]{2,1,0:T(8,128)(2,1)} %bitcast.3), calls=%async_computation | async-start | bytes 2097152 | tf_op jit(solution)/shard_map/all_to_all | solution.py:84
  150.3 0.2 all-reduce.5.cloned.1.call-start
  150.5 0.3 multiply_reduce_fusion
  150.8 0.2 multiply_convert_fusion.3
  151.1 30.3 %all-gather.5.cloned.1.call-done = bf16[1,2,1024,2048]{3,2,1,0:T(8,128)(2,1)} async-done(((bf16[1,2,256,2048]{3,2,1,0:T(8,128)(2,1)}), bf16[1,2,1024,2048]{3,2,1,0:T(8,128)(2,1)}) %all-gather.5.cloned.1.call-update) | async-done | bytes 8388624 | tf_op jit(solution)/shard_map/all_gather | solution.py:87
  181.4 6.5 %fusion.7 = f32[512,2048]{1,0:T(8,128)} fusion(bf16[512,1024]{1,0:T(8,128)(2,1)S(1)} %bitcast.99, bf16[1,2,1024,2048]{3,2,1,0:T(8,128)(2,1)} %all-gather.5.cloned.1.call-done), kind=kOutput, calls=%fused_computation.23 | convolution fusion | flops 2147483648 | bytes 9437184 | tf_op jit(solution)/shard_map/dot_general | solution.py:90
  187.9 6.6 %multiply_convert_fusion.1 = bf16[512,2048]{1,0:T(8,128)(2,1)S(1)} fusion(f32[512,2048]{1,0:T(8,128)} %fusion.7, bf16[512,1024]{1,0:T(8,128)(2,1)S(1)} %bitcast.94, bf16[1,2,1024,2048]{3,2,1,0:T(8,128)(2,1)} %all-gather.5.cloned.1.call-done), kind=kOutput, calls=%fused_computation.18 | convolution fusion | flops 2156920832 | bytes 11534336 | tf_op jit(solution)/shard_map/dot_general | solution.py:26
  194.5 1.3 copy-done.12
  195.9 3.4 fusion.17
  199.2 0.0 all-reduce.5.cloned.1.call-update
  199.2 0.3 reduce-scatter.5.cloned.1.call-start
  199.5 0.1 rsqrt.27
  199.6 6.7 %convert_bitcast_fusion = bf16[1,1024,2048]{2,1,0:T(8,128)(2,1)} fusion(bf16[512,1024]{1,0:T(8,128)(2,1)S(1)} %bitcast.95, f32[512,2048]{1,0:T(8,128)} %fusion.7), kind=kOutput, calls=%fused_computation.13 | convolution fusion | flops 2154823680 | bytes 9437184 | tf_op jit(solution)/shard_map/dot_general | solution.py:35
  206.3 19.7 %all-reduce.5.cloned.1.call-done = bf16[512,1024]{1,0:T(8,128)(2,1)} async-done(((bf16[512,1024]{1,0:T(8,128)(2,1)}), bf16[512,1024]{1,0:T(8,128)(2,1)}) %all-reduce.5.cloned.1.call-update) | async-done | bytes 1048592 | tf_op jit(solution)/shard_map/psum | solution.py:22
  225.9 1.8 fusion.16
  227.7 6.0 %convert_bitcast_fusion.1 = bf16[1,1024,2048]{2,1,0:T(8,128)(2,1)} fusion(bf16[512,1024]{1,0:T(8,128)(2,1)S(1)} %get-tuple-element.8, bf16[512,2048]{1,0:T(8,128)(2,1)} %copy-done.12), kind=kOutput, calls=%fused_computation.15 | convolution fusion | flops 2149580800 | bytes 7340032 | tf_op jit(solution)/shard_map/dot_general | solution.py:32
  233.7 7.5 %pad_maximum_fusion.1 = bf16[2,1024,2048]{2,1,0:T(8,128)(2,1)} fusion(bf16[1,1024,2048]{2,1,0:T(8,128)(2,1)} %convert_bitcast_fusion, bf16[1,1024,2048]{2,1,0:T(8,128)(2,1)} %convert_bitcast_fusion.1), kind=kLoop, calls=%fused_computation.1 | loop fusion | flops 4194304 | bytes 16777216 | tf_op jit(solution)/shard_map/stack | solution.py:38
  241.2 0.0 reduce-scatter.5.cloned.1.call-update
  241.2 0.0 reduce-scatter.3.cloned.1.call-start
  241.3 1.1 copy-done.1
  242.4 0.6 fusion.14
  243.0 22.3 %all_to_all.15 = bf16[16,32,1024]{2,1,0:T(8,128)(2,1)S(1)} all-to-all(bf16[16,32,1024]{2,1,0:T(8,128)(2,1)S(1)} %bitcast.96), channel_id=1, replica_groups=mesh['aa'=4,'ba'=16,'ma'=2] {'ba'}, dimensions={0} | all-to-all | bytes 2097152 | tf_op jit(solution)/shard_map/all_to_all | solution.py:102
  265.3 1.2 convolution_convert_fusion.2
  266.6 0.3 copy.25
  266.9 3.4 convert_bitcast_fusion.2
  270.3 6.9 %convert_bitcast_fusion.3 = bf16[1,1024,2048]{2,1,0:T(8,128)(2,1)} fusion(bf16[256,1024]{1,0:T(8,128)(2,1)S(1)} %copy-done.5, bf16[256,1024]{1,0:T(8,128)(2,1)S(1)} %bitcast.101, bf16[1,2,1024,2048]{3,2,1,0:T(8,128)(2,1)} %all-gather.3.cloned.1.call-done, f32[256,2048]{1,0:T(8,128)S(1)} %copy-done.11), kind=kOutput, calls=%fused_computation.17 | convolution fusion | flops 2154299392 | bytes 11534336 | tf_op jit(solution)/shard_map/dot_general | solution.py:32
  277.2 7.4 %pad_maximum_fusion = bf16[2,1024,2048]{2,1,0:T(8,128)(2,1)} fusion(bf16[1,1024,2048]{2,1,0:T(8,128)(2,1)} %convert_bitcast_fusion.2, bf16[1,1024,2048]{2,1,0:T(8,128)(2,1)} %convert_bitcast_fusion.3), kind=kLoop, calls=%fused_computation | loop fusion | flops 4194304 | bytes 16777216 | tf_op jit(solution)/shard_map/stack | solution.py:38
  284.6 0.0 reduce-scatter.3.cloned.1.call-update
  284.6 0.0 copy-start.2
  284.6 0.0 copy-start.3
  284.7 38.1 %reduce-scatter.5.cloned.1.call-done = bf16[2,256,2048]{2,1,0:T(8,128)(2,1)} async-done(((bf16[2,1024,2048]{2,1,0:T(8,128)(2,1)}), bf16[2,256,2048]{2,1,0:T(8,128)(2,1)}) %reduce-scatter.5.cloned.1.call-update) | async-done | bytes 2097168 | tf_op jit(solution)/shard_map/reduce_scatter | solution.py:117
  322.8 9.5 %fusion.3 = (f32[1,2,256,2048]{3,2,1,0:T(8,128)}, f32[1,2,256,2048]{3,2,1,0:T(8,128)}) fusion(f32[1,2,256,2048]{3,2,1,0:T(8,128)} %param.14, bf16[2,256,2048]{2,1,0:T(8,128)(2,1)} %reduce-scatter.5.cloned.1.call-done, f32[1,2,256,2048]{3,2,1,0:T(8,128)} %param.15), kind=kLoop, calls=%fused_computation.11 | loop fusion | flops 8388608 | bytes 18874368 | tf_op jit(solution)/shard_map/sub | solution.py:43
  332.3 77.0 %reduce-scatter.3.cloned.1.call-done = bf16[2,64,2048]{2,1,0:T(8,128)(2,1)} async-done(((bf16[2,1024,2048]{2,1,0:T(8,128)(2,1)}), bf16[2,64,2048]{2,1,0:T(8,128)(2,1)}) %reduce-scatter.3.cloned.1.call-update) | async-done | bytes 524304 | tf_op jit(solution)/shard_map/reduce_scatter | solution.py:114
  409.3 2.7 fusion.20
  (22 shorter events, 0.1 us)
Async XLA Ops:
  8.0 77.5 %all-gather.3.cloned.1.call-start = ((), (), s32[]{:S(2)}) async-start(), calls=%async_computation.5 | async-start | bytes 8912896 | tf_op jit(solution)/shard_map/all_gather | solution.py:68
  10.2 109.0 %all-reduce.3.cloned.1.call-start = ((), (), s32[]{:S(2)}) async-start(), calls=%async_computation.6 | async-start | bytes 1048576 | tf_op jit(solution)/shard_map/psum | solution.py:22
  88.9 1.3 copy-start.9
  94.5 4.1 copy-start.8
  94.5 24.6 %copy-start = (bf16[16,16,1024]{2,1,0:T(8,128)(2,1)S(1)}, bf16[16,16,1024]{2,1,0:T(8,128)(2,1)}, u32[]{:S(2)}) copy-start(bf16[16,16,1024]{2,1,0:T(8,128)(2,1)} %param.8) | copy-start | bytes 1572868
  94.6 86.8 %all-gather.5.cloned.1.call-start = ((), (), s32[]{:S(2)}) async-start(), calls=%async_computation.7 | async-start | bytes 10485760 | tf_op jit(solution)/shard_map/all_gather | solution.py:87
  98.5 31.5 %copy-start.6 = (s32[16]{0:T(128)S(1)}, s32[16]{0:T(128)}, u32[]{:S(2)}) copy-start(s32[16]{0:T(128)} %param.11) | copy-start | bytes 196
  98.5 31.5 %copy-start.4 = (bf16[16,16,1024]{2,1,0:T(8,128)(2,1)S(1)}, bf16[16,16,1024]{2,1,0:T(8,128)(2,1)}, u32[]{:S(2)}) copy-start(bf16[16,16,1024]{2,1,0:T(8,128)(2,1)} %param.9) | copy-start | bytes 1572868
  123.3 22.4 %all-to-all-start.1 = ((bf16[16,32,1024]{2,1,0:T(8,128)(2,1)}), bf16[16,32,1024]{2,1,0:T(8,128)(2,1)S(1)}, u32[]{:S(2)}, u32[]{:S(2)}) async-start(bf16[16,32,1024]{2,1,0:T(8,128)(2,1)} %bitcast.9), calls=%async_computation.1 | async-start | bytes 2097152 | tf_op jit(solution)/shard_map/all_to_all | solution.py:77
  145.8 42.2 %all-to-all-start = ((bf16[16,32,1024]{2,1,0:T(8,128)(2,1)}), bf16[16,32,1024]{2,1,0:T(8,128)(2,1)S(1)}, u32[]{:S(2)}, u32[]{:S(2)}) async-start(bf16[16,32,1024]{2,1,0:T(8,128)(2,1)} %bitcast.3), calls=%async_computation | async-start | bytes 2097152 | tf_op jit(solution)/shard_map/all_to_all | solution.py:84
  150.3 75.6 %all-reduce.5.cloned.1.call-start = ((), (), s32[]{:S(2)}) async-start(), calls=%async_computation.8 | async-start | bytes 2097152 | tf_op jit(solution)/shard_map/psum | solution.py:22
  187.9 7.9 %copy-start.7 = (bf16[1,2,1024,2048]{3,2,1,0:T(8,128)(2,1)S(1)}, bf16[1,2,1024,2048]{3,2,1,0:T(8,128)(2,1)}, u32[]{:S(2)}) copy-start(bf16[1,2,1024,2048]{3,2,1,0:T(8,128)(2,1)} %all-gather.5.cloned.1.call-done) | copy-start | bytes 25165828
  194.5 1.3 copy-start.12
  199.2 123.6 %reduce-scatter.5.cloned.1.call-start = ((), (), s32[]{:S(2)}) async-start(), calls=%async_computation.10 | async-start | bytes 10485760 | tf_op jit(solution)/shard_map/reduce_scatter | solution.py:117
  241.2 1.2 copy-start.1
  241.2 168.1 %reduce-scatter.3.cloned.1.call-start = ((), (), s32[]{:S(2)}) async-start(), calls=%async_computation.9 | async-start | bytes 8912896 | tf_op jit(solution)/shard_map/reduce_scatter | solution.py:114
  242.4 24.5 %copy-start.10 = (f32[256,2048]{1,0:T(8,128)S(1)}, f32[256,2048]{1,0:T(8,128)}, u32[]{:S(2)}) copy-start(f32[256,2048]{1,0:T(8,128)} %copy-done.9) | copy-start | bytes 6291460
  266.9 3.4 copy-start.5
  266.9 3.4 copy-start.11
  284.6 124.7 %copy-start.2 = (f32[1,2,64,2048]{3,2,1,0:T(8,128)S(1)}, f32[1,2,64,2048]{3,2,1,0:T(8,128)}, u32[]{:S(2)}) copy-start(f32[1,2,64,2048]{3,2,1,0:T(8,128)} %param.12) | copy-start | bytes 3145732
  284.6 124.7 %copy-start.3 = (f32[1,2,64,2048]{3,2,1,0:T(8,128)S(1)}, f32[1,2,64,2048]{3,2,1,0:T(8,128)}, u32[]{:S(2)}) copy-start(f32[1,2,64,2048]{3,2,1,0:T(8,128)} %param.13) | copy-start | bytes 3145732
Sparse Core Ops, SparseCore 0:
  11.6 73.8 all-gather.2
  94.6 24.4 all-reduce.2
  199.4 26.5 all-reduce.4
Sparse Core Ops, SparseCore 1:
  98.6 82.7 all-gather.4
  241.3 81.5 reduce-scatter.4
  326.1 83.2 reduce-scatter.2
where the time goes:
time: 421 us; the launch traced here: 419 us
  waiting for transfers between devices  272 us (65%)
  matrix products  49.5 us (12%)
  other arithmetic  40.8 us (10%)
  blocking collectives  22.3 us (5%)
  between operations  15.6 us (4%)
  starting transfers between devices  11.8 us (3%)
  local copies, waits for them, and re-layouts  7.38 us (2%)
    reduce_scatter x1, waiting for transfers between devices, local(): lax.psum_scatter(terms_one.astype(jnp.bfloat16), 'ba', scatter_dimension=...  77 us
    all_gather x1, waiting for transfers between devices, local(): lax.all_gather(wt1.astype(jnp.bfloat16), 'ba', axis=2, tiled=True)[0]  72.8 us
    psum x2, waiting for transfers between devices, join_halves(): lax.psum(partial_value.astype(jnp.bfloat16), 'ma').astype(jnp.float32)  40 us
    reduce_scatter x1, waiting for transfers between devices, local(): lax.psum_scatter(terms_two.astype(jnp.bfloat16), 'aa', scatter_dimension=...  38.1 us
    all_gather x1, waiting for transfers between devices, local(): lax.all_gather(wt2.astype(jnp.bfloat16), 'aa', axis=2, tiled=True)[0]  30.3 us
    all_to_all x1, blocking collectives, local(): lax.all_to_all(back_two.reshape(groups, SLOT * block, width), 'ba', split...  22.3 us
    another operation x2, other arithmetic, weight_terms(): return jnp.stack([first, second])  14.9 us
    all_to_all x1, waiting for transfers between devices, local(): lax.all_to_all(to_slots(output.reshape(blocks, block, width)), 'ba', spli...  13.5 us
  transfers between devices with their start and end apart: 8, of which 7 were waited for; matrix products, arithmetic and copies ran while one was open for 13% of the time, Pallas kernels for 0%

commit v1 on v0

v1 whole, which is shorter than its diff:
```python
import jax
import jax.numpy as jnp
from jax import lax
from jax.experimental import pallas as pl
from jax.experimental.pallas import tpu as pltpu
from jax.sharding import PartitionSpec as P

SLOT = 2
EPS = 1e-05
MOMENTUM = 0.9
OUTER_RATE = 0.7

MESH = pl.DeviceIdType.MESH
BF16 = jnp.bfloat16
F32 = jnp.float32
RING = 4
VMEM_LIMIT = 60 * 1024 * 1024


def dot(left, right, contract=(1, 0)):
    return lax.dot_general(
        left,
        right,
        (((contract[0],), (contract[1],)), ((), ())),
        preferred_element_type=F32,
    )


def wrap(index, size=RING):
    return lax.rem(index + size, size)


class Gather:
    def __init__(self, own, land, rank, device, send, recv):
        up, down = wrap(rank + 1), wrap(rank - 1)

        def copy(number, source, target, to):
            return pltpu.make_async_remote_copy(
                src_ref=source,
                dst_ref=target,
                send_sem=send.at[number],
                recv_sem=recv.at[number],
                device_id=device(to),
                device_id_type=MESH,
            )

        self.direct = [
            copy(0, own(0), land(rank, 0), up),
            copy(1, own(1), land(rank, 1), down),
            copy(2, own(1), land(rank, 1), up),
            copy(3, own(0), land(rank, 0), down),
        ]
        self.passed = [
            copy(4, land(down, 0), land(down, 0), up),
            copy(5, land(up, 1), land(up, 1), down),
        ]

    def start(self):
        for copy in self.direct:
            copy.start()

    def forward(self):
        for near, far in zip(self.direct[:2], self.passed):
            near.wait_recv()
            far.start()

    def near(self):
        for copy in self.direct[2:]:
            copy.wait_recv()

    def far(self):
        for copy in self.passed:
            copy.wait_recv()

    def drain(self):
        for copy in self.direct + self.passed:
            copy.wait_send()


class Scatter:
    def __init__(self, own, summed, bufs, rank, device, send, recv):
        up, down, far = wrap(rank + 1), wrap(rank - 1), wrap(rank + 2)
        through, landed = bufs

        def copy(number, source, target, to):
            return pltpu.make_async_remote_copy(
                src_ref=source,
                dst_ref=target,
                send_sem=send.at[number],
                recv_sem=recv.at[number],
                device_id=device(to),
                device_id_type=MESH,
            )

        self.first = [
            copy(0, own(far, 0), through.at[0], up),
            copy(1, own(far, 1), through.at[1], down),
            copy(2, own(up, 1), landed.at[1], up),
            copy(3, own(down, 0), landed.at[2], down),
        ]
        self.second = [
            copy(4, summed.at[0], landed.at[0], up),
            copy(5, summed.at[1], landed.at[3], down),
        ]
        self.through, self.summed, self.landed = through, summed, landed

    def start(self):
        for copy in self.first:
            copy.start()

    def forward(self, mine):
        for which in range(2):
            self.first[which].wait_recv()
            total = mine(which).astype(F32) + self.through[which].astype(F32)
            self.summed[which] = total.astype(BF16)
            self.second[which].start()

    def finish(self):
        for copy in self.first[2:] + self.second:
            copy.wait_recv()

    def total(self, half, mine):
        return mine.astype(F32) + (
            self.landed[half].astype(F32) + self.landed[2 + half].astype(F32)
        )

    def drain(self):
        for copy in self.first + self.second:
            copy.wait_send()


class Exchange:
    def __init__(self, packed, halves, place, send, recv, pair_send, pair_recv):
        level, base, core = place
        self.place, self.groups = place, packed.shape[0]
        self.packed, self.halves, self.send, self.recv = packed, halves, send, recv
        self.pair = pltpu.make_async_remote_copy(
            src_ref=halves.at[core],
            dst_ref=halves.at[core],
            send_sem=pair_send,
            recv_sem=pair_recv,
            device_id=(level, base, 1 - core),
            device_id_type=MESH,
        )

    def copy(self, step):
        level, base, core = self.place
        target = lax.rem(base + step, self.groups)
        return pltpu.make_async_remote_copy(
            src_ref=self.packed.at[target],
            dst_ref=self.halves.at[core, base],
            send_sem=self.send.at[step],
            recv_sem=self.recv.at[step],
            device_id=(level, target, core),
            device_id_type=MESH,
        )

    def start(self):
        level, base, core = self.place

        def step(number, carry):
            self.copy(number).start()
            return carry

        lax.fori_loop(1, self.groups, step, 0)
        self.halves[core, base] = self.packed[base]

    def turn(self):
        def step(number, carry):
            self.copy(number).wait_recv()
            return carry

        lax.fori_loop(1, self.groups, step, 0)
        self.pair.start()

    def finish(self):
        self.pair.wait_recv()

    def drain(self):
        def step(number, carry):
            self.copy(number).wait_send()
            return carry

        lax.fori_loop(1, self.groups, step, 0)
        self.pair.wait_send()


def greet(devices):
    barrier = pltpu.get_barrier_semaphore()
    for device in devices:
        pl.semaphore_signal(barrier, inc=1, device_id=device, device_id_type=MESH)
    pl.semaphore_wait(barrier, len(devices))


def here():
    level, base, core = lax.axis_index("aa"), lax.axis_index("ba"), lax.axis_index("ma")
    return level, base, core, base // RING, lax.rem(base, RING)


def rms(floated):
    width = floated.shape[-1]
    return lax.rsqrt(jnp.sum(floated * floated, axis=-1, keepdims=True) / width + EPS)


def forward_kernel(
    docs, masked, pick, own1, own2,
    down1, act_out, gate_out, terms_out, back_out,
    weights1, weights2, cot_send, cot, row_send, rows, back_send, back,
    normed1, act1, gate1, part1, part1_in,
    normed2, incoming2, act2, slopes2, dn, dn_in, terms2,
    ring_send, ring_recv, swap_send, swap_recv, pair_send, pair_recv, dn_send, dn_recv, local_sem,
):
    level, base, core, row, col = here()
    width, hidden = weights1.shape[2] * 16, weights1.shape[3]
    half, tile = width // 2, hidden // 4
    groups = cot_send.shape[0]
    deep, block = weights2.shape[2], weights1.shape[2]
    sibling = (level, base, 1 - core)
    greet(
        [sibling, (wrap(level + 1), base, core), (wrap(level - 1), base, core)]
        + [(level, lax.rem(base + step, groups), core) for step in range(1, groups)]
    )

    def at(matrix, along, other):
        return other * RING + along if matrix == 0 else along * RING + other

    def gather1(matrix, phase, shift, number):
        along, other = (col, row) if matrix == 0 else (row, col)
        h = block // 2
        if phase == 0:
            spot = lambda pos: at(matrix, pos, other)
            rank = along
        else:
            fixed = wrap(along + shift)
            spot = lambda pos: at(matrix, fixed, pos)
            rank = other
        land = lambda pos, part: weights1.at[matrix, spot(pos), pl.ds(part * h, h)]
        if phase == 0 or shift == 0:
            own = lambda part: own1.at[matrix, pl.ds(part * h, h)]
        else:
            own = lambda part: land(rank, part)
        device = lambda pos: (level, spot(pos) if phase == 0 else at(matrix, along, pos), core)
        return Gather(own, land, rank, device, ring_send.at[number], ring_recv.at[number])

    first = [gather1(m, 0, 0, m) for m in range(2)]
    second = [[gather1(m, 1, s, 2 + 4 * m + k) for k, s in enumerate((0, -1, 1, 2))] for m in range(2)]

    def gather2(matrix):
        h = deep // 2
        return Gather(
            lambda part: own2.at[matrix, pl.ds(part * h, h)],
            lambda pos, part: weights2.at[matrix, pos, pl.ds(part * h, h)],
            level,
            lambda pos: (pos, base, core),
            ring_send.at[10 + matrix],
            ring_recv.at[10 + matrix],
        )

    column = [gather2(m) for m in range(2)]
    for m in range(2):
        first[m].start()
    for m in (1, 0):
        column[m].start()
    for m in range(2):
        second[m][0].start()
    mine = [
        pltpu.make_async_copy(own1, weights1.at[:, base], local_sem.at[0]),
        pltpu.make_async_copy(own2, weights2.at[:, level], local_sem.at[1]),
    ]
    for copy in mine:
        copy.start()

    place = (level, base, core)
    left = pl.ds(pl.multiple_of(core * half, half), half)
    swaps = [
        Exchange(a, b, place, swap_send.at[k], swap_recv.at[k], pair_send.at[k], pair_recv.at[k])
        for k, (a, b) in enumerate(((cot_send, cot), (row_send, rows), (back_send, back)))
    ]
    cot_send[...] = dot(pick[...], masked[:, left]).astype(BF16).reshape(cot_send.shape)
    swaps[0].start()

    floated = docs[...].astype(F32)
    normed1[...] = (floated * rms(floated)).astype(BF16)

    for m in range(2):
        first[m].forward()
    for m in range(2):
        first[m].near()
        second[m][1].start()
        second[m][2].start()
    for m in range(2):
        first[m].far()
        second[m][3].start()
    for m in range(2):
        second[m][0].forward()
    column[1].forward()
    for k in (1, 2):
        for m in range(2):
            second[m][k].forward()
    swaps[0].turn()
    for m in range(2):
        second[m][3].forward()
    column[0].forward()
    for m in range(2):
        for k in range(4):
            second[m][k].near()
            second[m][k].far()
    mine[0].wait()

    keep_down = pltpu.make_async_copy(weights1.at[1], down1, local_sem.at[2])
    keep_down.start()

    def up_tile(number, carry):
        columns = pl.ds(pl.multiple_of(number * tile, tile), tile)
        pre = dot(normed1[...], weights1[0, :, :, columns].reshape(width, tile))
        sigma = jax.nn.sigmoid(pre)
        act1[:, columns] = (pre * sigma).astype(BF16)
        gate1[:, columns] = (sigma * (1.0 + pre * (1.0 - sigma))).astype(BF16)
        return carry

    lax.fori_loop(0, 4, up_tile, 0)
    keep = [
        pltpu.make_async_copy(act1, act_out, local_sem.at[3]),
        pltpu.make_async_copy(gate1, gate_out, local_sem.at[4]),
    ]
    for copy in keep:
        copy.start()

    def down_tile(number, carry):
        piece = weights1[1, pl.ds(number * 4, 4)].reshape(4 * block, hidden)
        part1[number] = dot(act1[...], piece, (1, 1)).astype(BF16)
        return carry

    lax.fori_loop(0, 4, down_tile, 0)
    give = pltpu.make_async_remote_copy(
        src_ref=part1.at[pl.ds(2 * (1 - core), 2)],
        dst_ref=part1_in,
        send_sem=dn_send.at[4],
        recv_sem=dn_recv.at[4],
        device_id=sibling,
        device_id_type=MESH,
    )
    give.start()
    give.wait_recv()
    quarter = half // 2
    for k in range(2):
        columns = pl.ds(pl.multiple_of(core * half + k * quarter, quarter), quarter)
        total = part1[2 * core + k].astype(F32) + part1_in[k].astype(F32)
        output = (docs[:, columns].astype(F32) + total).astype(BF16)
        row_send[:, :, k * quarter:(k + 1) * quarter] = (
            dot(pick[...], output).astype(BF16).reshape(groups, -1, quarter)
        )
    swaps[1].start()
    swaps[0].finish()

    count = cot.shape[1] * cot.shape[2]
    side = lambda ref, h: ref[h].reshape(count, half)

    def piece2(matrix, h, columns):
        return weights2[matrix, 2 * h:2 * h + 2, :, columns].reshape(half, tile)

    mine[1].wait()
    column[1].near()
    column[1].far()

    def incoming_tile(number, carry):
        columns = pl.ds(pl.multiple_of(number * tile, tile), tile)
        incoming2[:, columns] = dot(side(cot, 0), piece2(1, 0, columns)) + dot(
            side(cot, 1), piece2(1, 1, columns)
        )
        return carry

    lax.fori_loop(0, 4, incoming_tile, 0)
    swaps[1].turn()
    swaps[1].finish()
    floats = [side(rows, h).astype(F32) for h in range(2)]
    square = sum(jnp.sum(f * f, axis=-1, keepdims=True) for f in floats)
    factor = lax.rsqrt(square / width + EPS)
    for h in range(2):
        normed2[h] = (side(rows, h).astype(F32) * factor).astype(BF16)
    column[0].near()
    column[0].far()

    def slope_tile(number, carry):
        columns = pl.ds(pl.multiple_of(number * tile, tile), tile)
        pre = dot(normed2[0], piece2(0, 0, columns)) + dot(normed2[1], piece2(0, 1, columns))
        sigma = jax.nn.sigmoid(pre)
        act2[:, columns] = (pre * sigma).astype(BF16)
        slopes2[:, columns] = (
            incoming2[:, columns] * sigma * (1.0 + pre * (1.0 - sigma))
        ).astype(BF16)
        return carry

    lax.fori_loop(0, 4, slope_tile, 0)

    def dn_copy(number):
        return pltpu.make_async_remote_copy(
            src_ref=dn.at[number],
            dst_ref=dn_in.at[number],
            send_sem=dn_send.at[number],
            recv_sem=dn_recv.at[number],
            device_id=sibling,
            device_id_type=MESH,
        )

    def dn_tile(number, carry):
        dn[number] = dot(slopes2[...], weights2[0, number], (1, 1)).astype(BF16)
        dn_copy(number).start()
        return carry

    lax.fori_loop(0, 4, dn_tile, 0)

    def term_tile(matrix, lefts, right):
        def step(number, carry):
            columns = pl.ds(pl.multiple_of(number * tile, tile), tile)
            for h in range(2):
                terms2[matrix, h * half:(h + 1) * half, columns] = dot(
                    lefts(h), right[:, columns], (0, 0)
                ).astype(BF16)
            return carry

        lax.fori_loop(0, 4, step, 0)
        copy = pltpu.make_async_copy(
            terms2.at[matrix], terms_out.at[matrix], local_sem.at[5 + matrix]
        )
        copy.start()
        return copy

    keep.append(term_tile(1, lambda h: side(cot, h), act2))
    for number in range(4):
        dn_copy(number).wait_recv()

    def dn_of(number):
        return dn[number].astype(F32) + dn_in[number].astype(F32)

    mean = jnp.zeros((count, 1), F32)
    for number in range(4):
        columns = slice((number % 2) * quarter, (number % 2 + 1) * quarter)
        normed = rows[number // 2, :, :, columns].reshape(count, quarter).astype(F32) * factor
        mean = mean + jnp.sum(dn_of(number) * normed, axis=-1, keepdims=True)
    mean = mean / width
    for k in range(2):
        columns = slice(k * quarter, (k + 1) * quarter)
        normed = rows[core, :, :, columns].reshape(count, quarter).astype(F32) * factor
        value = cot[core, :, :, columns].reshape(count, quarter).astype(F32) + factor * (
            dn_of(2 * core + k) - normed * mean
        )
        back_send[:, :, columns] = value.astype(BF16).reshape(groups, -1, quarter)
    swaps[2].start()
    keep.append(term_tile(0, lambda h: normed2[h], slopes2))
    swaps[2].turn()
    swaps[2].finish()
    keep.append(pltpu.make_async_copy(back, back_out, local_sem.at[7]))
    keep[-1].start()

    for gather in first + second[0] + second[1] + column:
        gather.drain()
    for swap in swaps:
        swap.drain()
    give.wait_send()
    for number in range(4):
        dn_copy(number).wait_send()
    keep_down.wait()
    for copy in keep:
        copy.wait()


def backward_kernel(
    docs, pick, down1, act1, gate1, terms2, back,
    sum1, sum2,
    weights1, normed1, upstream, slopes, terms1, own2,
    through, summed, landed, mid, through_b, summed_b, landed_b,
    send, recv, local_sem,
):
    level, base, core, row, col = here()
    width, hidden = docs.shape[1], act1.shape[1]
    half, tile = width // 2, hidden // 4
    block = width // 16
    neighbours = [(wrap(level + s), base, core) for s in (1, -1)]
    neighbours += [(level, wrap(row + s) * RING + col, core) for s in (1, -1)]
    neighbours += [(level, row * RING + wrap(col + s), core) for s in (1, -1)]
    load = pltpu.make_async_copy(down1, weights1, local_sem.at[0])
    load.start()
    h2 = width // 8

    def part2(matrix, pos, part):
        return terms2.at[matrix, pos, pl.ds(part * 2, 2)]

    loads = []
    for m in range(2):
        loads.append(
            [
                pltpu.make_async_copy(part2(m, wrap(level + 1), 0), summed.at[m, 0], local_sem.at[1 + 3 * m]),
                pltpu.make_async_copy(part2(m, wrap(level - 1), 1), summed.at[m, 1], local_sem.at[2 + 3 * m]),
                pltpu.make_async_copy(terms2.at[m, level], own2.at[m], local_sem.at[3 + 3 * m]),
            ]
        )
        for copy in loads[m]:
            copy.start()
    greet(neighbours)

    def scatter2(matrix):
        return Scatter(
            lambda pos, part: part2(matrix, pos, part),
            summed.at[matrix],
            (through.at[matrix], landed.at[matrix]),
            level,
            lambda pos: (pos, base, core),
            send.at[matrix],
            recv.at[matrix],
        )

    column = [scatter2(m) for m in range(2)]
    for scatter in column:
        scatter.start()

    count = back.shape[1] * back.shape[2]
    for h in range(2):
        upstream[h] = dot(pick[...], back[h].reshape(count, half), (0, 0)).astype(BF16)
    floated = docs[...].astype(F32)
    normed1[...] = (floated * rms(floated)).astype(BF16)

    def term_tile(matrix, left, right):
        def step(number, carry):
            columns = pl.ds(pl.multiple_of(number * tile, tile), tile)
            for h in range(2):
                value = dot(left(h), right[:, columns], (0, 0)).astype(BF16)
                terms1[matrix, 2 * h:2 * h + 2, :, :, columns] = value.reshape(2, RING, block, tile)
            return carry

        lax.fori_loop(0, 4, step, 0)

    def part1(matrix, pos, part):
        if matrix == 0:
            return terms1.at[0, pos, pl.ds(part * 2, 2)]
        return terms1.at[1, pl.ds(part * 2, 2), pos]

    def scatter1(matrix):
        if matrix == 0:
            rank, device = row, lambda pos: (level, pos * RING + col, core)
        else:
            rank, device = col, lambda pos: (level, row * RING + pos, core)
        return Scatter(
            lambda pos, part: part1(matrix, pos, part),
            summed.at[2 + matrix],
            (through.at[2 + matrix], landed.at[2 + matrix]),
            rank,
            device,
            send.at[2 + matrix],
            recv.at[2 + matrix],
        )

    plane = [scatter1(m) for m in range(2)]
    term_tile(1, lambda h: upstream[h], act1)
    plane[1].start()
    load.wait()

    def slope_tile(number, carry):
        columns = pl.ds(pl.multiple_of(number * tile, tile), tile)
        incoming = dot(upstream[0], weights1[0:8, :, columns].reshape(half, tile)) + dot(
            upstream[1], weights1[8:16, :, columns].reshape(half, tile)
        )
        slopes[:, columns] = (incoming * gate1[:, columns].astype(F32)).astype(BF16)
        return carry

    lax.fori_loop(0, 4, slope_tile, 0)
    term_tile(0, lambda h: normed1[:, h * half:(h + 1) * half], slopes)
    plane[0].start()

    for m in range(2):
        for copy in loads[m]:
            copy.wait()
    column[0].forward(lambda which: summed[0, which])
    ranks = (row, col)

    def mine1(matrix, pos, part):
        return part1(matrix, pos, part)[...]

    for m in (1, 0):
        plane[m].forward(
            lambda which, m=m: mine1(m, wrap(ranks[m] + 1 - 2 * which), which)
        )
    column[1].forward(lambda which: summed[1, which])

    def scatter_b(matrix):
        if matrix == 0:
            rank, device = col, lambda pos: (level, row * RING + pos, core)
        else:
            rank, device = row, lambda pos: (level, pos * RING + col, core)
        hb = block // 2
        return Scatter(
            lambda pos, part: mid.at[matrix, pos, pl.ds(part * hb, hb)],
            summed_b.at[matrix],
            (through_b.at[matrix], landed_b.at[matrix]),
            rank,
            device,
            send.at[4 + matrix],
            recv.at[4 + matrix],
        )

    last = [scatter_b(m) for m in range(2)]
    for m in (1, 0):
        plane[m].finish()
        for part in range(2):
            mid[m, 2 * part:2 * part + 2] = plane[m].total(part, mine1(m, ranks[m], part)).astype(BF16)
        last[m].start()
    other = (col, row)
    hb = block // 2
    for m in (1, 0):
        last[m].forward(
            lambda which, m=m: mid[m, wrap(other[m] + 1 - 2 * which), pl.ds(which * hb, hb)]
        )
    for m in (1, 0):
        last[m].finish()
        for part in range(2):
            mine = mid[m, other[m], pl.ds(part * hb, hb)]
            sum1[m, part * hb:(part + 1) * hb] = last[m].total(part, mine).astype(BF16)
    for m in range(2):
        column[m].finish()
        for part in range(2):
            mine = own2[m, 2 * part:2 * part + 2]
            sum2[m, 2 * part:2 * part + 2] = column[m].total(part, mine).astype(BF16)
    for scatter in column + plane + last:
        scatter.drain()


def outer_step(weights, moment, delta):
    new_moment = MOMENTUM * moment + delta[None]
    return (weights - OUTER_RATE * (delta[None] + MOMENTUM * new_moment), new_moment)


def local(docs, cot, route, doc_len, wt1, mom1, wt2, mom2):
    blocks, block, width = docs.shape
    groups = lax.axis_size("ba")
    levels = lax.axis_size("aa")
    slots = groups * SLOT
    count, lanes = slots * block, blocks * block
    hidden = wt1.shape[-1]
    inside = lax.broadcasted_iota(jnp.int32, (blocks, block), 1) < doc_len[:, None]
    masked = jnp.where(inside[:, :, None], cot, jnp.zeros_like(cot)).reshape(lanes, width)
    targets = route[:, 0]
    shared = targets[:, None] == targets[None, :]
    before = lax.broadcasted_iota(jnp.int32, (blocks, blocks), 0) > lax.broadcasted_iota(
        jnp.int32, (blocks, blocks), 1
    )
    rank = jnp.sum((shared & before).astype(jnp.int32), axis=1)
    target_row = (targets * SLOT + rank)[:, None] * block + jnp.arange(block, dtype=jnp.int32)[None]
    pick = (
        lax.broadcasted_iota(jnp.int32, (count, lanes), 0) == target_row.reshape(1, lanes)
    ).astype(BF16)
    rows = docs.reshape(lanes, width)

    def shape(*sizes, kind=BF16):
        return jax.ShapeDtypeStruct(sizes, kind)

    whole = pl.BlockSpec(memory_space=pltpu.VMEM)
    anywhere = pl.BlockSpec(memory_space=pl.ANY)
    half, quarter = width // 2, width // 4
    per = count // groups
    swap = [pltpu.VMEM((groups, per, half), BF16), pltpu.VMEM((2, groups, per, half), BF16)]
    down1, act1, gate1, terms2, back = pl.pallas_call(
        forward_kernel,
        out_shape=(
            shape(16, width // 16, hidden),
            shape(lanes, hidden),
            shape(lanes, hidden),
            shape(2, width, hidden),
            shape(2, groups, per, half),
        ),
        in_specs=[whole, whole, whole, anywhere, anywhere],
        out_specs=[anywhere] * 5,
        scratch_shapes=[
            pltpu.VMEM((2, 16, width // 16, hidden), BF16),
            pltpu.VMEM((2, RING, width // 4, hidden), BF16),
        ]
        + swap * 3
        + [
            pltpu.VMEM((lanes, width), BF16),
            pltpu.VMEM((lanes, hidden), BF16),
            pltpu.VMEM((lanes, hidden), BF16),
            pltpu.VMEM((RING, lanes, quarter), BF16),
            pltpu.VMEM((2, lanes, quarter), BF16),
            pltpu.VMEM((2, count, half), BF16),
            pltpu.VMEM((count, hidden), F32),
            pltpu.VMEM((count, hidden), BF16),
            pltpu.VMEM((count, hidden), BF16),
            pltpu.VMEM((RING, count, quarter), BF16),
            pltpu.VMEM((RING, count, quarter), BF16),
            pltpu.VMEM((2, width, hidden), BF16),
            pltpu.SemaphoreType.DMA((12, 6)),
            pltpu.SemaphoreType.DMA((12, 6)),
            pltpu.SemaphoreType.DMA((3, groups)),
            pltpu.SemaphoreType.DMA((3, groups)),
            pltpu.SemaphoreType.DMA((3,)),
            pltpu.SemaphoreType.DMA((3,)),
            pltpu.SemaphoreType.DMA((5,)),
            pltpu.SemaphoreType.DMA((5,)),
            pltpu.SemaphoreType.DMA((8,)),
        ],
        compiler_params=pltpu.CompilerParams(
            collective_id=0, has_side_effects=True, vmem_limit_bytes=VMEM_LIMIT
        ),
        name="forward",
    )(rows, masked, pick, wt1[0].astype(BF16), wt2[0].astype(BF16))

    group = width // 4
    unit = group // 4
    sum1, sum2 = pl.pallas_call(
        backward_kernel,
        out_shape=(shape(2, width // 16, hidden), shape(2, 4, unit, hidden)),
        in_specs=[whole, whole, anywhere, whole, whole, anywhere, whole],
        out_specs=[whole, whole],
        scratch_shapes=[
            pltpu.VMEM((16, width // 16, hidden), BF16),
            pltpu.VMEM((lanes, width), BF16),
            pltpu.VMEM((2, lanes, half), BF16),
            pltpu.VMEM((lanes, hidden), BF16),
            pltpu.VMEM((2, RING, RING, width // 16, hidden), BF16),
            pltpu.VMEM((2, 4, unit, hidden), BF16),
            pltpu.VMEM((4, 2, 2, unit, hidden), BF16),
            pltpu.VMEM((4, 2, 2, unit, hidden), BF16),
            pltpu.VMEM((4, 4, 2, unit, hidden), BF16),
            pltpu.VMEM((2, RING, width // 16, hidden), BF16),
            pltpu.VMEM((2, 2, width // 32, hidden), BF16),
            pltpu.VMEM((2, 2, width // 32, hidden), BF16),
            pltpu.VMEM((2, 4, width // 32, hidden), BF16),
            pltpu.SemaphoreType.DMA((6, 6)),
            pltpu.SemaphoreType.DMA((6, 6)),
            pltpu.SemaphoreType.DMA((7,)),
        ],
        compiler_params=pltpu.CompilerParams(
            collective_id=1, has_side_effects=True, vmem_limit_bytes=VMEM_LIMIT
        ),
        name="backward",
    )(rows, pick, down1, act1, gate1, terms2.reshape(2, RING, 4, unit, hidden), back)
    delta1 = sum1.astype(F32) / groups
    delta2 = sum2.reshape(2, group, hidden).astype(F32) / levels
    new_wt1, new_mom1 = outer_step(wt1, mom1, delta1)
    new_wt2, new_mom2 = outer_step(wt2, mom2, delta2)
    return (new_wt1, new_mom1, new_wt2, new_mom2)


def solution(mesh):
    return jax.shard_map(
        local,
        mesh=mesh,
        in_specs=(
            P(("aa", "ba"), None, None),
            P(("aa", "ba"), None, None),
            P(("aa", "ba"), None),
            P(("aa", "ba")),
            P("aa", None, "ba", "ma"),
            P("aa", None, "ba", "ma"),
            P("ba", None, "aa", "ma"),
            P("ba", None, "aa", "ma"),
        ),
        out_specs=(
            P("aa", None, "ba", "ma"),
            P("aa", None, "ba", "ma"),
            P("ba", None, "aa", "ma"),
            P("ba", None, "aa", "ma"),
        ),
        check_vma=False,
    )
```

time: 421 us -> 201 us (0.48)
  waiting for transfers between devices: 272 us -> 0 us
  Pallas kernels: 0 us -> 179 us
  matrix products: 49.5 us -> 0 us
  blocking collectives: 22.3 us -> 0 us
  other arithmetic: 40.8 us -> 19.3 us
  between operations: 15.6 us -> 0.71 us
  starting transfers between devices: 11.8 us -> 0 us
  local copies, waits for them, and re-layouts: 7.38 us -> 1.94 us
    pallas_call x0 -> x2, Pallas kernels: none -> 179 us  [the longest x1 102 us: local(): pl.pallas_call(forward_kernel, out_shape=(shape(16, width // 16, hidden),...]
    reduce_scatter x2 -> x0, waiting for transfers between devices: 115 us -> none  [the longest x1 77 us: local(): lax.psum_scatter(terms_one.astype(jnp.bfloat16), 'ba', scatter_dimension=...]
    all_gather x2 -> x0, waiting for transfers between devices: 103 us -> none  [the longest x1 72.8 us: local(): lax.all_gather(wt1.astype(jnp.bfloat16), 'ba', axis=2, tiled=True)[0]]
    dot_general x12 -> x0, matrix products: 49.5 us -> none  [the longest x2 12.9 us: weight_terms(): lax.dot_general(normed_low, slopes, (((0,), (0,)), ((), ())), preferred_e...]
    psum x2 -> x0, waiting for transfers between devices: 40 us -> none  [join_halves(): lax.psum(partial_value.astype(jnp.bfloat16), 'ma').astype(jnp.float32)]
    all_to_all x1 -> x0, blocking collectives: 22.3 us -> none  [local(): lax.all_to_all(back_two.reshape(groups, SLOT * block, width), 'ba', split...]
    another operation x2 -> x0, other arithmetic: 14.9 us -> none  [weight_terms(): return jnp.stack([first, second])]
    all_to_all x2 -> x0, waiting for transfers between devices: 13.5 us -> none  [the longest x1 13.5 us: local(): lax.all_to_all(to_slots(output.reshape(blocks, block, width)), 'ba', spli...]
  transfers between devices with their start and end apart: 8 -> 0, of which waited for: 7 -> 0; matrix products, arithmetic and copies ran while one was open for 13% -> 0% of each run, Pallas kernels for 0% -> 0%
where the time goes in v1:
time: 201 us
  Pallas kernels  179 us (89%)
  other arithmetic  19.3 us (10%)
    pallas_call x1, Pallas kernels, local(): pl.pallas_call(forward_kernel, out_shape=(shape(16, width // 16, hidden),...  102 us
    pallas_call x1, Pallas kernels, local(): pl.pallas_call(backward_kernel, out_shape=(shape(2, width // 16, hidden),...  76.3 us
    sub x2, other arithmetic, outer_step(): weights - OUTER_RATE * (delta[None] + MOMENTUM * new_moment)  7.78 us

profile of v1, /device:TPU:1, one launch (start us, length us, event | category | flops | bytes accessed | tf_op | source)
XLA Modules:
  0.0 200.7 jit_solution(6722642573948476024)
XLA Ops:
  0.6 0.9 convert_reduce_fusion
  1.5 0.7 fusion.5
  2.2 0.7 iota_compare_fusion.1
  2.9 0.1 iota_add_fusion
  3.0 0.1 add.43
  3.1 0.8 fusion.2.pick
  3.9 1.9 broadcast_select_fusion
  5.8 2.1 %convert_bitcast_fusion.1.own1 = bf16[2,64,2048]{2,1,0:T(8,128)(2,1)} fusion(f32[1,2,64,2048]{3,2,1,0:T(8,128)} %param.12), kind=kLoop, calls=%fused_computation.9 | loop fusion | flops 262144 | bytes 1572864 | tf_op jit(solution)/shard_map/convert_element_type | solution.py:704
  7.9 3.8 %convert_bitcast_fusion.own2 = bf16[2,256,2048]{2,1,0:T(8,128)(2,1)} fusion(f32[1,2,256,2048]{3,2,1,0:T(8,128)} %param.14), kind=kLoop, calls=%fused_computation.3 | loop fusion | flops 1048576 | bytes 6291456 | tf_op jit(solution)/shard_map/convert_element_type | solution.py:704
  11.7 102.4 %forward.1 = (bf16[16,64,2048]{2,1,0:T(8,128)(2,1)}, bf16[256,2048]{1,0:T(8,128)(2,1)}, bf16[256,2048]{1,0:T(8,128)(2,1)}, bf16[2,1024,2048]{2,1,0:T(8,128)(2,1)}, bf16[2,16,32,512]{3,2,1,0:T(8,128)(2,1)}) custom-call(bf16[256,1024]{1,0:T(8,128)(2,1)} %bitcast.27, bf16[256,1024]{1,0:T(8,128)(2,1)} %bitcast.29, bf16[512,256]{1,0:T(8,128)(2,1)} %fusion.2.pick, ...), custom_call_target="tpu_custom_call" | custom-call | tf_op jit(solution)/shard_map/forward/pallas_call | solution.py:661
  114.2 0.0 copy-start.2
  114.2 0.0 copy-start.4
  114.2 76.3 %backward.1 = (bf16[2,64,2048]{2,1,0:T(8,128)(2,1)}, bf16[2,4,64,2048]{3,2,1,0:T(8,128)(2,1)}) custom-call(bf16[256,1024]{1,0:T(8,128)(2,1)} %bitcast.28, bf16[512,256]{1,0:T(8,128)(2,1)} %fusion.2.pick, bf16[16,64,2048]{2,1,0:T(8,128)(2,1)} %get-tuple-element.11.down1, bf16[256,2048]{1,0:T(8,128)(2,1)} %get-tuple-element.12.act1, ...), custom_call_target="tpu_custom_call" | custom-call | tf_op jit(solution)/shard_map/backward/pallas_call | solution.py:708
  190.4 0.0 copy-start.3
  190.5 0.0 copy-done.2
  190.5 0.0 copy-done.4
  190.5 0.0 copy-start.1
  190.5 2.9 %fusion.1 = (f32[1,2,64,2048]{3,2,1,0:T(8,128)}, f32[1,2,64,2048]{3,2,1,0:T(8,128)}) fusion(f32[1,2,64,2048]{3,2,1,0:T(8,128)S(1)} %copy-done.2, bf16[2,64,2048]{2,1,0:T(8,128)(2,1)} %get-tuple-element.16, f32[1,2,64,2048]{3,2,1,0:T(8,128)S(1)} %copy-done.4), kind=kLoop, calls=%fused_computation.7 | loop fusion | flops 2097152 | bytes 4718592 | tf_op jit(solution)/shard_map/sub | solution.py:629
  193.4 0.0 copy-start
  193.4 0.0 copy-done.3
  193.4 0.5 convert_multiply_fusion
  193.9 0.2 copy-done.1
  194.2 1.6 copy-done
  195.8 4.9 %multiply_subtract_fusion = (f32[1,2,256,2048]{3,2,1,0:T(8,128)}, f32[1,2,256,2048]{3,2,1,0:T(8,128)}) fusion(f32[1,2,256,2048]{3,2,1,0:T(8,128)S(1)} %copy-done, f32[1,2,256,2048]{3,2,1,0:T(8,128)S(1)} %bitcast.25, f32[1,2,256,2048]{3,2,1,0:T(8,128)S(1)} %copy-done.1), kind=kLoop, calls=%fused_computation | loop fusion | flops 6291456 | bytes 20971520 | tf_op jit(solution)/shard_map/sub | solution.py:629
Async XLA Ops:
  114.2 76.3 %copy-start.2 = (f32[1,2,64,2048]{3,2,1,0:T(8,128)S(1)}, f32[1,2,64,2048]{3,2,1,0:T(8,128)}, u32[]{:S(2)}) copy-start(f32[1,2,64,2048]{3,2,1,0:T(8,128)} %param.12) | copy-start | bytes 3145732
  114.2 76.3 %copy-start.4 = (f32[1,2,64,2048]{3,2,1,0:T(8,128)S(1)}, f32[1,2,64,2048]{3,2,1,0:T(8,128)}, u32[]{:S(2)}) copy-start(f32[1,2,64,2048]{3,2,1,0:T(8,128)} %param.13) | copy-start | bytes 3145732
  190.4 3.0 %copy-start.3 = (bf16[2,4,64,2048]{3,2,1,0:T(8,128)(2,1)S(1)}, bf16[2,4,64,2048]{3,2,1,0:T(8,128)(2,1)}, u32[]{:S(2)}) copy-start(bf16[2,4,64,2048]{3,2,1,0:T(8,128)(2,1)} %get-tuple-element.17) | copy-start | bytes 6291460
  190.5 3.7 %copy-start.1 = (f32[1,2,256,2048]{3,2,1,0:T(8,128)S(1)}, f32[1,2,256,2048]{3,2,1,0:T(8,128)}, u32[]{:S(2)}) copy-start(f32[1,2,256,2048]{3,2,1,0:T(8,128)} %param.15) | copy-start | bytes 12582916
  193.4 2.4 %copy-start = (f32[1,2,256,2048]{3,2,1,0:T(8,128)S(1)}, f32[1,2,256,2048]{3,2,1,0:T(8,128)}, u32[]{:S(2)}) copy-start(f32[1,2,256,2048]{3,2,1,0:T(8,128)} %param.14) | copy-start | bytes 12582916

commit v2 on v0

v2 whole, which is shorter than its diff:
```python
import jax
import jax.numpy as jnp
from jax import lax
from jax.experimental import pallas as pl
from jax.experimental.pallas import tpu as pltpu
from jax.sharding import PartitionSpec as P

SLOT = 2
EPS = 1e-05
MOMENTUM = 0.9
OUTER_RATE = 0.7

MESH = pl.DeviceIdType.MESH
BF16 = jnp.bfloat16
F32 = jnp.float32
RING = 4
VMEM_LIMIT = 57 * 1024 * 1024


def dot(left, right, contract=(1, 0)):
    return lax.dot_general(
        left,
        right,
        (((contract[0],), (contract[1],)), ((), ())),
        preferred_element_type=F32,
    )


def wrap(index, size=RING):
    return lax.rem(index + size, size)


def remote(source, target, send, recv, device):
    return pltpu.make_async_remote_copy(
        src_ref=source,
        dst_ref=target,
        send_sem=send,
        recv_sem=recv,
        device_id=device,
        device_id_type=MESH,
    )


def each(first, last, step):
    def body(number, carry):
        step(number)
        return carry

    lax.fori_loop(first, last, body, 0)


class Gather:
    def __init__(self, own, land, rank, device, send, recv):
        up, down = wrap(rank + 1), wrap(rank - 1)

        def copy(number, source, target, to):
            return remote(source, target, send.at[number], recv.at[number], device(to))

        self.direct = [
            copy(0, own(0), land(rank, 0), up),
            copy(1, own(1), land(rank, 1), down),
            copy(2, own(1), land(rank, 1), up),
            copy(3, own(0), land(rank, 0), down),
        ]
        self.passed = [
            copy(4, land(down, 0), land(down, 0), up),
            copy(5, land(up, 1), land(up, 1), down),
        ]

    def start(self):
        for copy in self.direct:
            copy.start()

    def forward(self):
        for near, far in zip(self.direct[:2], self.passed):
            near.wait_recv()
            far.start()

    def near(self):
        for copy in self.direct[2:]:
            copy.wait_recv()

    def far(self):
        for copy in self.passed:
            copy.wait_recv()

    def drain(self):
        for copy in self.direct + self.passed:
            copy.wait_send()


class Scatter:
    def __init__(self, own, bufs, rank, device, send, recv):
        up, down, far = wrap(rank + 1), wrap(rank - 1), wrap(rank + 2)
        through, summed, landed = bufs

        def copy(number, source, target, to):
            return remote(source, target, send.at[number], recv.at[number], device(to))

        self.first = [
            copy(0, own(far, 0), through.at[0], up),
            copy(1, own(far, 1), through.at[1], down),
            copy(2, own(up, 1), landed.at[1], up),
            copy(3, own(down, 0), landed.at[2], down),
        ]
        self.second = [
            copy(4, summed.at[0], landed.at[0], up),
            copy(5, summed.at[1], landed.at[3], down),
        ]
        self.through, self.summed, self.landed = through, summed, landed
        self.own, self.rank = own, rank

    def start(self):
        for copy in self.first:
            copy.start()

    def forward(self):
        for which in range(2):
            self.first[which].wait_recv()
            mine = self.own(wrap(self.rank + 1 - 2 * which), which)[...]
            total = mine.astype(F32) + self.through[which].astype(F32)
            self.summed[which] = total.astype(BF16)
            self.second[which].start()

    def finish(self):
        for copy in self.first[2:] + self.second:
            copy.wait_recv()

    def total(self, half):
        return self.own(self.rank, half)[...].astype(F32) + (
            self.landed[half].astype(F32) + self.landed[2 + half].astype(F32)
        )

    def drain(self):
        for copy in self.first + self.second:
            copy.wait_send()


class Exchange:
    def __init__(self, packed, land, place, send, recv):
        self.place, self.groups = place, packed.shape[0]
        self.packed, self.land, self.send, self.recv = packed, land, send, recv

    def copy(self, step):
        level, base, core = self.place
        target = lax.rem(base + step, self.groups)
        return remote(
            self.packed.at[target],
            self.land.at[base],
            self.send.at[step],
            self.recv.at[step],
            (level, target, core),
        )

    def start(self):
        each(1, self.groups, lambda step: self.copy(step).start())
        base = self.place[1]
        self.land[base] = self.packed[base]

    def wait(self, step):
        self.copy(step).wait_recv()

    def drain(self):
        each(1, self.groups, lambda step: self.copy(step).wait_send())


class Share:
    def __init__(self, exchange, rows, place, partner, sibling, send, recv, last_send, last_recv):
        core = place[2]
        self.exchange, self.groups = exchange, exchange.groups

        def copy(path, step):
            source = wrap(place[1] - step, self.groups)
            mine = rows.at[0, core, source]
            if path == 0:
                return remote(mine, mine, send.at[0, step], recv.at[0, step], sibling)
            return remote(mine, rows.at[1, core, source], send.at[1, step], recv.at[1, step], partner)

        self.copy = copy
        self.last = remote(rows.at[1, core], rows.at[1, core], last_send, last_recv, sibling)

    def turn(self):
        def step(number):
            self.copy(1, number).start()
            self.copy(0, number).start()

        def arrived(number):
            self.exchange.wait(number)
            step(number)

        step(0)
        each(1, self.groups, arrived)

    def own(self):
        each(0, self.groups, lambda step: self.copy(0, step).wait_recv())

    def partner(self):
        each(0, self.groups, lambda step: self.copy(1, step).wait_recv())
        self.last.start()

    def finish(self):
        self.last.wait_recv()

    def drain(self):
        def step(number):
            self.copy(0, number).wait_send()
            self.copy(1, number).wait_send()

        each(0, self.groups, step)
        self.last.wait_send()


def greet(devices):
    barrier = pltpu.get_barrier_semaphore()
    for device in devices:
        pl.semaphore_signal(barrier, inc=1, device_id=device, device_id_type=MESH)
    pl.semaphore_wait(barrier, len(devices))


def rms_of(square, width):
    return lax.rsqrt(square / width + EPS)


def kernel(
    docs, masked, pick, wt1, wt2,
    sum1, sum2,
    stage1, stage2, own1, own2, weights1, weights2,
    normed1, act1, gate1, part1, joined1, through1, summed1, landed1, out1,
    packed, cot, rows, back,
    normed2, act2, slopes2, dn_sum, dn_far, mean_out, mean_in,
    terms2, near2, via2, far2,
    upstream, terms1, through_x, summed_x, landed_x, mid, final1,
    ring_send, ring_recv, swap_send, swap_recv, share_send, share_recv, pair_send, pair_recv,
    col_send, col_recv, local_sem,
):
    level, base, core = lax.axis_index("aa"), lax.axis_index("ba"), lax.axis_index("ma")
    row, col = base // RING, lax.rem(base, RING)
    lanes, width = docs.shape
    groups = packed.shape[0]
    count = groups * packed.shape[1]
    half, quarter = width // 2, width // 4
    block, deep = weights1.shape[2], weights2.shape[2]
    hidden1, hidden2 = weights1.shape[3], weights2.shape[3]
    tile = hidden2 // 2
    mate, partner = level + 1 - 2 * lax.rem(level, 2), RING - 1 - level
    across = RING - 1 - mate
    side = level // 2
    place = (level, base, core)
    sibling = (level, base, 1 - core)
    mate_chip, partner_chip = (mate, base, core), (partner, base, core)

    loads = [
        pltpu.make_async_copy(wt1, stage1, local_sem.at[0]),
    ] + [
        pltpu.make_async_copy(
            wt2.at[m, :, pl.ds(h * hidden2, hidden2)], stage2.at[h, m], local_sem.at[1 + 2 * m + h]
        )
        for m in range(2)
        for h in range(2)
    ]
    for load in loads:
        load.start()
    greet(
        [sibling, mate_chip, partner_chip]
        + [(level, lax.rem(base + step, groups), core) for step in range(1, groups)]
    )

    loads[0].wait()
    for q in range(RING):
        for m in range(2):
            own1[q, m] = stage1[m, :, q * hidden1:(q + 1) * hidden1].astype(BF16)
    weights1[base] = own1[col]

    def along(step):
        other = wrap(col + step)
        return remote(
            own1.at[other],
            weights1.at[base],
            col_send.at[step],
            col_recv.at[step],
            (level, row * RING + other, core),
        )

    def gather_x(step, number):
        fixed = wrap(col + step)
        land = lambda pos, m: weights1.at[pos * RING + fixed, m]
        own = (lambda m: own1.at[col, m]) if step == 0 else (lambda m: land(row, m))
        device = lambda pos: (level, pos * RING + col, core)
        return Gather(own, land, row, device, ring_send.at[number], ring_recv.at[number])

    spread = [along(step) for step in (1, 3, 2)]
    gathers = [gather_x(step, k) for k, step in enumerate((0, 3, 1, 2))]
    for copy in spread:
        copy.start()
    gathers[0].start()

    rows_half = lanes // 2
    rows_part = rows_half // 2
    on_y = lambda pos: (level, row * RING + pos, core)

    def doc_part(pos, part):
        return normed1.at[pos, pl.ds(pl.multiple_of(core * rows_half + part * rows_part, rows_part), rows_part)]

    documents = Gather(
        lambda part: docs.at[pl.ds(pl.multiple_of(core * rows_half + part * rows_part, rows_part), rows_part)],
        doc_part,
        col,
        on_y,
        ring_send.at[4],
        ring_recv.at[4],
    )
    documents.start()

    def doc_pair(step):
        where = normed1.at[wrap(col + step), pl.ds(pl.multiple_of(core * rows_half, rows_half), rows_half)]
        return remote(where, where, pair_send.at[step], pair_recv.at[step], sibling)

    def down_z(m):
        return [
            remote(own2.at[1 - side, m], weights2.at[level, m], col_send.at[4 + m], col_recv.at[4 + m], partner_chip),
            remote(own2.at[side, m], weights2.at[level, m], col_send.at[6 + m], col_recv.at[6 + m], mate_chip),
            remote(weights2.at[partner, m], weights2.at[partner, m], col_send.at[8 + m], col_recv.at[8 + m], mate_chip),
        ]

    column = [down_z(m) for m in range(2)]
    for m in (1, 0):
        for h in range(2):
            loads[1 + 2 * m + h].wait()
            own2[h, m] = stage2[h, m].astype(BF16)
        column[m][0].start()
        column[m][1].start()
        weights2[level, m] = own2[side, m]

    left = pl.ds(pl.multiple_of(core * half, half), half)
    swaps = [
        Exchange(packed, land, place, swap_send.at[k], swap_recv.at[k])
        for k, land in enumerate((cot.at[0, core], rows.at[0, core], back))
    ]
    shares = [
        Share(
            swaps[k], buf, place, partner_chip, sibling,
            share_send.at[k], share_recv.at[k], pair_send.at[4 + k], pair_recv.at[4 + k],
        )
        for k, buf in enumerate((cot, rows))
    ]
    packed[...] = dot(pick[...], masked[:, left]).astype(BF16).reshape(packed.shape)
    swaps[0].start()

    for k, copy in enumerate((spread[0], spread[1], spread[2])):
        copy.wait_recv()
        gathers[1 + k].start()
    documents.forward()
    gathers[0].forward()
    documents.near()
    doc_pair(3).start()
    doc_pair(1).start()
    gathers[1].forward()
    gathers[2].forward()
    column[1][0].wait_recv()
    column[1][2].start()
    documents.far()
    doc_pair(2).start()
    gathers[3].forward()
    normed1[col] = docs[...]
    documents.drain()
    for step in (1, 2, 3):
        doc_pair(step).wait()

    def normalize_one(number):
        floated = normed1[number].astype(F32)
        square = jnp.sum(floated * floated, axis=-1, keepdims=True)
        normed1[number] = (floated * rms_of(square, width)).astype(BF16)

    each(0, RING, normalize_one)
    for gather in gathers:
        gather.near()
        gather.far()

    def matrix1(m):
        return weights1[:, m].reshape(width, hidden1)

    def give1(pos):
        return remote(
            part1.at[pos, 1 - core], joined1.at[pos], share_send.at[2, 0, pos], share_recv.at[2, 0, pos], sibling
        )

    def level_one(number):
        pos = lax.rem(col + 2 + 3 * number, RING)
        pre = dot(normed1[pos], matrix1(0))
        sigma = jax.nn.sigmoid(pre)
        active = (pre * sigma).astype(BF16)
        act1[pos] = active
        gate1[pos] = (sigma * (1.0 + pre * (1.0 - sigma))).astype(BF16)
        for h in range(2):
            piece = weights1[8 * h:8 * h + 8, 1].reshape(half, hidden1)
            part1[pos, h] = dot(active, piece, (1, 1)).astype(BF16)
        give1(pos).start()

    each(0, RING, level_one)

    def join_one(number):
        pos = lax.rem(col + 2 + 3 * number, RING)
        give1(pos).wait_recv()
        joined1[pos] = (part1[pos, core].astype(F32) + joined1[pos].astype(F32)).astype(BF16)

    each(0, RING, join_one)
    hold = lanes // 2
    reduce1 = Scatter(
        lambda pos, part: joined1.at[pos, pl.ds(part * hold, hold)],
        (through1, summed1, landed1),
        col,
        on_y,
        ring_send.at[5],
        ring_recv.at[5],
    )
    reduce1.start()
    column[0][0].wait_recv()
    column[0][2].start()
    reduce1.forward()
    shares[0].turn()
    reduce1.finish()
    for part in range(2):
        where = slice(part * hold, (part + 1) * hold)
        out1[where] = (docs[where, left].astype(F32) + reduce1.total(part)).astype(BF16)
    swaps[0].drain()
    packed[...] = dot(pick[...], out1[...]).astype(BF16).reshape(packed.shape)
    swaps[1].start()
    shares[0].own()
    shares[0].partner()

    def flat(ref, path, h):
        return ref[path, h].reshape(count, half)

    def piece2(m, h, columns):
        return weights2[2 * h:2 * h + 2, m, :, columns].reshape(half, tile)

    def columns_of(number):
        return pl.ds(pl.multiple_of(number * tile, tile), tile)

    column[1][1].wait_recv()
    column[1][2].wait_recv()
    shares[0].finish()

    def incoming_tile(number):
        path, columns = number // 2, columns_of(lax.rem(number, 2))
        value = dot(flat(cot, path, 0), piece2(1, 0, columns)) + dot(
            flat(cot, path, 1), piece2(1, 1, columns)
        )
        stage2[path, :, :, columns] = value.reshape(2, deep, tile)

    each(0, 4, incoming_tile)
    reduce1.drain()
    each(0, RING, lambda pos: give1(pos).wait_send())
    shares[1].turn()
    shares[1].own()

    def normalize_two(path):
        square = sum(
            jnp.sum(jnp.square(flat(rows, path, h).astype(F32)), axis=-1, keepdims=True) for h in range(2)
        )
        factor = rms_of(square, width)
        for h in range(2):
            normed2[path, h] = (flat(rows, path, h).astype(F32) * factor).astype(BF16)
        return factor

    def slope_tile(path):
        def step(number):
            columns = columns_of(number)
            pre = dot(normed2[path, 0], piece2(0, 0, columns)) + dot(normed2[path, 1], piece2(0, 1, columns))
            sigma = jax.nn.sigmoid(pre)
            incoming = stage2[path, :, :, columns].reshape(count, tile)
            act2[path, :, columns] = (pre * sigma).astype(BF16)
            slopes2[path, :, columns] = (incoming * sigma * (1.0 + pre * (1.0 - sigma))).astype(BF16)

        return step

    factor = normalize_two(0)
    column[0][1].wait_recv()
    column[0][2].wait_recv()
    each(0, 2, slope_tile(0))
    shares[1].partner()
    shares[1].finish()
    normalize_two(1)
    each(0, 2, slope_tile(1))

    def give2(path):
        where = pl.ds(2 * path, 2)
        return remote(
            part1.at[where, 1 - core], joined1.at[where], pair_send.at[6 + path], pair_recv.at[6 + path], sibling
        )

    def dn_tiles(path):
        def step(number):
            h = lax.rem(1 - core + number, 2)
            piece = weights2[pl.ds(2 * h, 2), 0].reshape(half, hidden2)
            value = dot(slopes2[path], piece, (1, 1)).astype(BF16)
            part1[2 * path:2 * path + 2, h] = value.reshape(2, lanes, half)

        each(0, 1, step)
        give2(path).start()
        each(1, 2, step)

    def dn_of(path):
        where = slice(2 * path, 2 * path + 2)
        return (part1[where, core].astype(F32) + joined1[where].astype(F32)).reshape(count, half)

    to_partner = remote(dn_sum, dn_far, pair_send.at[8], pair_recv.at[8], partner_chip)
    dn_tiles(1)
    give2(1).wait_recv()
    dn_sum[...] = dn_of(1).astype(BF16)
    to_partner.start()
    dn_tiles(0)

    def term_tiles(m, lefts, right):
        def step(number):
            columns = columns_of(number)
            for h in range(2):
                value = dot(lefts(0, h), right[0, :, columns], (0, 0)) + dot(
                    lefts(1, h), right[1, :, columns], (0, 0)
                )
                terms2[2 * h:2 * h + 2, m, :, columns] = value.astype(BF16).reshape(2, deep, tile)

        each(0, 2, step)

    def sums_z(m):
        return [
            remote(terms2.at[across, m], via2.at[m], col_send.at[10 + m], col_recv.at[10 + m], mate_chip),
            remote(terms2.at[mate, m], near2.at[m], col_send.at[12 + m], col_recv.at[12 + m], mate_chip),
            remote(via2.at[m], far2.at[m], col_send.at[14 + m], col_recv.at[14 + m], partner_chip),
        ]

    sums = [sums_z(m) for m in range(2)]
    term_tiles(1, lambda path, h: flat(cot, path, h), act2)
    sums[1][0].start()
    sums[1][1].start()

    give2(0).wait_recv()
    to_partner.wait_recv()

    def pieces():
        return flat(rows, 0, core).astype(F32) * factor, dn_of(0) + dn_far[...].astype(F32)

    normed, value = pieces()
    mean = jnp.sum(value * normed, axis=-1, keepdims=True)
    mean_out[...] = jnp.broadcast_to(mean, mean_out.shape)
    swap_mean = remote(mean_out, mean_in, pair_send.at[9], pair_recv.at[9], sibling)
    swap_mean.start()
    swap_mean.wait_recv()
    mean = (mean + mean_in[:, 0:1]) / width
    normed, value = pieces()
    result = flat(cot, 0, core).astype(F32) + factor * (value - normed * mean)
    swaps[1].drain()
    packed[...] = result.astype(BF16).reshape(packed.shape)
    swaps[2].start()
    term_tiles(0, lambda path, h: normed2[path, h], slopes2)
    sums[0][0].start()
    sums[0][1].start()
    sums[1][0].wait_recv()
    via2[1] = (terms2[partner, 1].astype(F32) + via2[1].astype(F32)).astype(BF16)
    sums[1][2].start()

    each(1, groups, swaps[2].wait)
    upstream[col, core] = dot(pick[...], back[...].reshape(count, half), (0, 0)).astype(BF16)
    lifts = Gather(
        lambda part: upstream.at[col, core, pl.ds(part * hold, hold)],
        lambda pos, part: upstream.at[pos, core, pl.ds(part * hold, hold)],
        col,
        on_y,
        ring_send.at[6],
        ring_recv.at[6],
    )
    lifts.start()

    def lift_pair(step):
        where = upstream.at[wrap(col + step), core]
        return remote(where, where, pair_send.at[10 + step], pair_recv.at[10 + step], sibling)

    lift_pair(0).start()
    lifts.forward()
    lifts.near()
    lift_pair(3).start()
    lift_pair(1).start()

    def slope_one(step):
        pos = wrap(col + step)
        lift_pair(step).wait_recv()
        incoming = dot(upstream[pos, 0], weights1[0:8, 1].reshape(half, hidden1)) + dot(
            upstream[pos, 1], weights1[8:16, 1].reshape(half, hidden1)
        )
        joined1[pos] = (incoming * gate1[pos].astype(F32)).astype(BF16)

    slope_one(0)
    lifts.far()
    lift_pair(2).start()
    slope_one(3)
    slope_one(1)
    slope_one(2)

    def term_one(m, lefts, right):
        for h in range(2):
            value = dot(lefts(h).reshape(RING * lanes, half), right[...].reshape(RING * lanes, hidden1), (0, 0))
            terms1[2 * h:2 * h + 2, m] = value.astype(BF16).reshape(2, RING, block, hidden1)

    def scatter_x(m):
        return Scatter(
            lambda pos, part: terms1.at[pos, m, pl.ds(2 * part, 2)],
            (through_x.at[m], summed_x.at[m], landed_x.at[m]),
            row,
            lambda pos: (level, pos * RING + col, core),
            ring_send.at[7 + m],
            ring_recv.at[7 + m],
        )

    plane = [scatter_x(m) for m in range(2)]
    term_one(1, lambda h: upstream[:, h], act1)
    plane[1].start()
    term_one(0, lambda h: normed1[:, :, h * half:(h + 1) * half], joined1)
    plane[0].start()
    plane[1].forward()
    sums[0][0].wait_recv()
    via2[0] = (terms2[partner, 0].astype(F32) + via2[0].astype(F32)).astype(BF16)
    sums[0][2].start()
    plane[0].forward()

    def along_back(step):
        other = wrap(col + step)
        return remote(
            mid.at[other], final1.at[col], col_send.at[16 + step], col_recv.at[16 + step],
            (level, row * RING + other, core),
        )

    for m in (1, 0):
        plane[m].finish()
        for part in range(2):
            mid[2 * part:2 * part + 2, m] = plane[m].total(part).astype(BF16)
    for step in (2, 1, 3):
        along_back(step).start()
    final1[col] = mid[col]
    own_side = pl.ds(pl.multiple_of(side * hidden2, hidden2), hidden2)
    other_side = pl.ds(pl.multiple_of((1 - side) * hidden2, hidden2), hidden2)
    for m in (1, 0):
        sums[m][1].wait_recv()
        sum2[m, :, own_side] = (terms2[level, m].astype(F32) + near2[m].astype(F32)).astype(BF16)
        sums[m][2].wait_recv()
        sum2[m, :, other_side] = far2[m]
    for step in (1, 3, 2):
        along_back(step).wait_recv()
    for q in range(RING):
        sum1[:, :, q * hidden1:(q + 1) * hidden1] = final1[q]

    for copy in spread + column[0] + column[1] + sums[0] + sums[1]:
        copy.wait_send()
    for ring in gathers + [lifts] + plane + [swaps[2]] + shares:
        ring.drain()
    for step in range(RING):
        lift_pair(step).wait_send()
    for step in (1, 2, 3):
        along_back(step).wait_send()
    give2(0).wait_send()
    give2(1).wait_send()
    to_partner.wait_send()
    swap_mean.wait_send()


def outer_step(weights, moment, delta):
    new_moment = MOMENTUM * moment + delta[None]
    return (weights - OUTER_RATE * (delta[None] + MOMENTUM * new_moment), new_moment)


def local(docs, cot, route, doc_len, wt1, mom1, wt2, mom2):
    blocks, block, width = docs.shape
    groups = lax.axis_size("ba")
    levels = lax.axis_size("aa")
    slots = groups * SLOT
    count, lanes = slots * block, blocks * block
    hidden = wt1.shape[-1]
    inside = lax.broadcasted_iota(jnp.int32, (blocks, block), 1) < doc_len[:, None]
    masked = jnp.where(inside[:, :, None], cot, jnp.zeros_like(cot)).reshape(lanes, width)
    targets = route[:, 0]
    shared = targets[:, None] == targets[None, :]
    before = lax.broadcasted_iota(jnp.int32, (blocks, blocks), 0) > lax.broadcasted_iota(
        jnp.int32, (blocks, blocks), 1
    )
    rank = jnp.sum((shared & before).astype(jnp.int32), axis=1)
    target_row = (targets * SLOT + rank)[:, None] * block + jnp.arange(block, dtype=jnp.int32)[None]
    pick = (
        lax.broadcasted_iota(jnp.int32, (count, lanes), 0) == target_row.reshape(1, lanes)
    ).astype(BF16)
    rows = docs.reshape(lanes, width)

    whole = pl.BlockSpec(memory_space=pltpu.VMEM)
    anywhere = pl.BlockSpec(memory_space=pl.ANY)
    half, quarter = width // 2, width // 4
    per = count // groups
    small = width // 16
    hidden1, hidden2 = hidden // RING, hidden // 2

    def vmem(*sizes, kind=BF16):
        return pltpu.VMEM(sizes, kind)

    def dma(*sizes):
        return pltpu.SemaphoreType.DMA(sizes)

    hold = lanes // 2
    sum1, sum2 = pl.pallas_call(
        kernel,
        out_shape=(
            jax.ShapeDtypeStruct((2, small, hidden), BF16),
            jax.ShapeDtypeStruct((2, quarter, hidden), BF16),
        ),
        in_specs=[whole, whole, whole, anywhere, anywhere],
        out_specs=[whole, whole],
        scratch_shapes=[
            vmem(2, small, hidden, kind=F32),
            vmem(2, 2, quarter, hidden2, kind=F32),
            vmem(RING, 2, small, hidden1),
            vmem(2, 2, quarter, hidden2),
            vmem(16, 2, small, hidden1),
            vmem(RING, 2, quarter, hidden2),
            vmem(RING, lanes, width),
            vmem(RING, lanes, hidden1),
            vmem(RING, lanes, hidden1),
            vmem(RING, 2, lanes, half),
            vmem(RING, lanes, half),
            vmem(2, hold, half),
            vmem(2, hold, half),
            vmem(4, hold, half),
            vmem(lanes, half),
            vmem(groups, per, half),
            vmem(2, 2, groups, per, half),
            vmem(2, 2, groups, per, half),
            vmem(groups, per, half),
            vmem(2, 2, count, half),
            vmem(2, count, hidden2),
            vmem(2, count, hidden2),
            vmem(count, half),
            vmem(count, half),
            vmem(count, 128, kind=F32),
            vmem(count, 128, kind=F32),
            vmem(RING, 2, quarter, hidden2),
            vmem(2, quarter, hidden2),
            vmem(2, quarter, hidden2),
            vmem(2, quarter, hidden2),
            vmem(RING, 2, lanes, half),
            vmem(RING, 2, RING, small, hidden1),
            vmem(2, 2, 2, small, hidden1),
            vmem(2, 2, 2, small, hidden1),
            vmem(2, 4, 2, small, hidden1),
            vmem(RING, 2, small, hidden1),
            vmem(RING, 2, small, hidden1),
            dma(9, 6),
            dma(9, 6),
            dma(3, groups),
            dma(3, groups),
            dma(3, 2, groups),
            dma(3, 2, groups),
            dma(14),
            dma(14),
            dma(20),
            dma(20),
            dma(5),
        ],
        compiler_params=pltpu.CompilerParams(
            collective_id=0, has_side_effects=True, vmem_limit_bytes=VMEM_LIMIT
        ),
        name="window",
    )(rows, masked, pick, wt1[0], wt2[0])

    delta1 = sum1.astype(F32) / groups
    delta2 = sum2.astype(F32) / levels
    new_wt1, new_mom1 = outer_step(wt1, mom1, delta1)
    new_wt2, new_mom2 = outer_step(wt2, mom2, delta2)
    return (new_wt1, new_mom1, new_wt2, new_mom2)


def solution(mesh):
    return jax.shard_map(
        local,
        mesh=mesh,
        in_specs=(
            P(("aa", "ba"), None, None),
            P(("aa", "ba"), None, None),
            P(("aa", "ba"), None),
            P(("aa", "ba")),
            P("aa", None, "ba", "ma"),
            P("aa", None, "ba", "ma"),
            P("ba", None, "aa", "ma"),
            P("ba", None, "aa", "ma"),
        ),
        out_specs=(
            P("aa", None, "ba", "ma"),
            P("aa", None, "ba", "ma"),
            P("ba", None, "aa", "ma"),
            P("ba", None, "aa", "ma"),
        ),
        check_vma=False,
    )
```

time: 421 us -> 172 us (0.41)
  waiting for transfers between devices: 272 us -> 0 us
  Pallas kernels: 0 us -> 156 us
  matrix products: 49.5 us -> 0 us
  other arithmetic: 40.8 us -> 15.1 us
  blocking collectives: 22.3 us -> 0 us
  between operations: 15.6 us -> 0.68 us
  starting transfers between devices: 11.8 us -> 0 us
  local copies, waits for them, and re-layouts: 7.38 us -> 0.1 us
    pallas_call x0 -> x1, Pallas kernels: none -> 156 us  [local(): pl.pallas_call(kernel, out_shape=(jax.ShapeDtypeStruct((2, small, hidden)...]
    reduce_scatter x2 -> x0, waiting for transfers between devices: 115 us -> none  [the longest x1 77 us: local(): lax.psum_scatter(terms_one.astype(jnp.bfloat16), 'ba', scatter_dimension=...]
    all_gather x2 -> x0, waiting for transfers between devices: 103 us -> none  [the longest x1 72.8 us: local(): lax.all_gather(wt1.astype(jnp.bfloat16), 'ba', axis=2, tiled=True)[0]]
    dot_general x12 -> x0, matrix products: 49.5 us -> none  [the longest x2 12.9 us: weight_terms(): lax.dot_general(normed_low, slopes, (((0,), (0,)), ((), ())), preferred_e...]
    psum x2 -> x0, waiting for transfers between devices: 40 us -> none  [join_halves(): lax.psum(partial_value.astype(jnp.bfloat16), 'ma').astype(jnp.float32)]
    all_to_all x1 -> x0, blocking collectives: 22.3 us -> none  [local(): lax.all_to_all(back_two.reshape(groups, SLOT * block, width), 'ba', split...]
    another operation x2 -> x0, other arithmetic: 14.9 us -> none  [weight_terms(): return jnp.stack([first, second])]
    all_to_all x2 -> x0, waiting for transfers between devices: 13.5 us -> none  [the longest x1 13.5 us: local(): lax.all_to_all(to_slots(output.reshape(blocks, block, width)), 'ba', spli...]
  transfers between devices with their start and end apart: 8 -> 0, of which waited for: 7 -> 0; matrix products, arithmetic and copies ran while one was open for 13% -> 0% of each run, Pallas kernels for 0% -> 0%
where the time goes in v2:
time: 172 us
  Pallas kernels  156 us (91%)
  other arithmetic  15.1 us (9%)
    pallas_call x1, Pallas kernels, local(): pl.pallas_call(kernel, out_shape=(jax.ShapeDtypeStruct((2, small, hidden)...  156 us
    sub x2, other arithmetic, outer_step(): weights - OUTER_RATE * (delta[None] + MOMENTUM * new_moment)  10 us

profile of v2, /device:TPU:1, one launch (start us, length us, event | category | flops | bytes accessed | tf_op | source)
XLA Modules:
  0.0 171.5 jit_solution(124763981044503665)
XLA Ops:
  0.6 0.7 iota_compare_fusion.2
  1.4 1.9 %broadcast_select_fusion = bf16[16,16,1024]{2,1,0:T(8,128)(2,1)} fusion(bf16[16,16,1024]{2,1,0:T(8,128)(2,1)} %param.9, pred[16,16]{1,0:T(8,128)(4,1)S(1)} %iota_compare_fusion.2), kind=kLoop, calls=%fused_computation.12 | loop fusion | flops 262144 | bytes 1048832 | tf_op jit(solution)/shard_map/jit(_where)/select_n | solution.py:678
  3.3 0.9 convert_reduce_fusion
  4.2 0.7 fusion.7
  4.9 0.1 iota_add_fusion
  5.0 0.1 add.43
  5.0 0.0 copy-start
  5.0 0.8 fusion.4.pick
  5.8 155.6 %window.1 = (bf16[2,64,2048]{2,1,0:T(8,128)(2,1)}, bf16[2,256,2048]{2,1,0:T(8,128)(2,1)}) custom-call(bf16[256,1024]{1,0:T(8,128)(2,1)} %bitcast.32, bf16[256,1024]{1,0:T(8,128)(2,1)} %bitcast.31, bf16[512,256]{1,0:T(8,128)(2,1)} %fusion.4.pick, f32[2,64,2048]{2,1,0:T(8,128)} %bitcast.30, f32[2,256,2048]{2,1,0:T(8,128)} %bitcast.29), custom_call_target="tpu_custom_call" | custom-call | tf_op jit(solution)/shard_map/window/pallas_call | solution.py:705
  161.4 0.0 copy-done
  161.4 0.0 copy-start.1
  161.4 0.0 copy-start.2
  161.5 0.0 copy-start.3
  161.5 8.4 %fusion.1 = (f32[1,2,256,2048]{3,2,1,0:T(8,128)}, f32[1,2,256,2048]{3,2,1,0:T(8,128)}) fusion(f32[1,2,256,2048]{3,2,1,0:T(8,128)S(1)} %copy-done, bf16[2,256,2048]{2,1,0:T(8,128)(2,1)} %get-tuple-element.7, f32[1,2,256,2048]{3,2,1,0:T(8,128)} %param.15), kind=kLoop, calls=%fused_computation.3 | loop fusion | flops 8388608 | bytes 18874368 | tf_op jit(solution)/shard_map/sub | solution.py:667
  169.9 0.0 copy-done.1
  169.9 0.0 copy-done.2
  169.9 0.0 copy-done.3
  169.9 1.6 fusion.3
Async XLA Ops:
  5.0 156.4 %copy-start = (f32[1,2,256,2048]{3,2,1,0:T(8,128)S(1)}, f32[1,2,256,2048]{3,2,1,0:T(8,128)}, u32[]{:S(2)}) copy-start(f32[1,2,256,2048]{3,2,1,0:T(8,128)} %param.14) | copy-start | bytes 12582916
  161.4 8.5 %copy-start.1 = (f32[1,2,64,2048]{3,2,1,0:T(8,128)S(1)}, f32[1,2,64,2048]{3,2,1,0:T(8,128)}, u32[]{:S(2)}) copy-start(f32[1,2,64,2048]{3,2,1,0:T(8,128)} %param.12) | copy-start | bytes 3145732
  161.4 8.5 %copy-start.2 = (f32[1,2,64,2048]{3,2,1,0:T(8,128)S(1)}, f32[1,2,64,2048]{3,2,1,0:T(8,128)}, u32[]{:S(2)}) copy-start(f32[1,2,64,2048]{3,2,1,0:T(8,128)} %param.13) | copy-start | bytes 3145732
  161.5 8.5 %copy-start.3 = (bf16[2,64,2048]{2,1,0:T(8,128)(2,1)S(1)}, bf16[2,64,2048]{2,1,0:T(8,128)(2,1)}, u32[]{:S(2)}) copy-start(bf16[2,64,2048]{2,1,0:T(8,128)(2,1)} %get-tuple-element.6) | copy-start | bytes 1572868

commit v3 on v2

--- a/solution.py
+++ b/solution.py
@@ -217,13 +217,42 @@
     pl.semaphore_wait(barrier, len(devices))
 
 
+def doc_of_row(lanes, docs):
+    row = lax.broadcasted_iota(jnp.int32, (lanes, docs), 0) // (lanes // docs)
+    return (row == lax.broadcasted_iota(jnp.int32, (lanes, docs), 1)).astype(F32)
+
+
+def slot_matrix(route, pick):
+    count, lanes = pick.shape
+    docs = route.shape[0]
+    block = lanes // docs
+    target = route[...].astype(F32)
+    spread = jnp.broadcast_to(target, (docs, 128))
+    by_row = dot(spread, doc_of_row(lanes, docs), (0, 1))[0:docs]
+    own = lax.broadcasted_iota(jnp.int32, (docs, lanes), 1)
+    earlier = lax.broadcasted_iota(jnp.int32, (docs, lanes), 0) < own // block
+    rank = jnp.sum(jnp.where((by_row == target) & earlier, 1.0, 0.0), axis=0, keepdims=True)
+    place = (by_row[0:1] * SLOT + rank) * block + lax.rem(own[0:1], block).astype(F32)
+    slots = lax.broadcasted_iota(jnp.int32, (count, lanes), 0).astype(F32)
+    pick[...] = jnp.where(slots == place, 1.0, 0.0).astype(BF16)
+
+
+def live_rows(doc_len, lanes):
+    docs = doc_len.shape[1]
+    lengths = jnp.broadcast_to(doc_len[...].astype(F32), (128, docs))
+    lengths = dot(doc_of_row(lanes, docs), lengths, (1, 1))[:, 0:1]
+    position = lax.rem(lax.broadcasted_iota(jnp.int32, (lanes, 1), 0), lanes // docs)
+    return position.astype(F32) < lengths
+
+
 def rms_of(square, width):
     return lax.rsqrt(square / width + EPS)
 
 
 def kernel(
-    docs, masked, pick, wt1, wt2,
+    docs, cot_docs, route, doc_len, wt1, wt2,
     sum1, sum2,
+    pick,
     stage1, stage2, own1, own2, weights1, weights2,
     normed1, act1, gate1, part1, joined1, through1, summed1, landed1, out1,
     packed, cot, rows, back,
@@ -309,8 +338,6 @@
         ring_send.at[4],
         ring_recv.at[4],
     )
-    documents.start()
-
     def doc_pair(step):
         where = normed1.at[wrap(col + step), pl.ds(pl.multiple_of(core * rows_half, rows_half), rows_half)]
         return remote(where, where, pair_send.at[step], pair_recv.at[step], sibling)
@@ -343,24 +370,26 @@
         )
         for k, buf in enumerate((cot, rows))
     ]
-    packed[...] = dot(pick[...], masked[:, left]).astype(BF16).reshape(packed.shape)
-    swaps[0].start()
+    slot_matrix(route, pick)
+    live = live_rows(doc_len, lanes)
+    masked = jnp.where(live, cot_docs[:, left], jnp.zeros((lanes, half), BF16))
+    packed[...] = dot(pick[...], masked).astype(BF16).reshape(packed.shape)
 
     for k, copy in enumerate((spread[0], spread[1], spread[2])):
         copy.wait_recv()
         gathers[1 + k].start()
+    documents.start()
+    for gather in gathers[:3]:
+        gather.forward()
+    column[1][0].wait_recv()
+    column[1][2].start()
+    gathers[3].forward()
     documents.forward()
-    gathers[0].forward()
     documents.near()
     doc_pair(3).start()
     doc_pair(1).start()
-    gathers[1].forward()
-    gathers[2].forward()
-    column[1][0].wait_recv()
-    column[1][2].start()
     documents.far()
     doc_pair(2).start()
-    gathers[3].forward()
     normed1[col] = docs[...]
     documents.drain()
     for step in (1, 2, 3):
@@ -375,6 +404,7 @@
     for gather in gathers:
         gather.near()
         gather.far()
+    swaps[0].start()
 
     def matrix1(m):
         return weights1[:, m].reshape(width, hidden1)
@@ -426,7 +456,6 @@
     packed[...] = dot(pick[...], out1[...]).astype(BF16).reshape(packed.shape)
     swaps[1].start()
     shares[0].own()
-    shares[0].partner()
 
     def flat(ref, path, h):
         return ref[path, h].reshape(count, half)
@@ -439,7 +468,6 @@
 
     column[1][1].wait_recv()
     column[1][2].wait_recv()
-    shares[0].finish()
 
     def incoming_tile(number):
         path, columns = number // 2, columns_of(lax.rem(number, 2))
@@ -448,10 +476,11 @@
         )
         stage2[path, :, :, columns] = value.reshape(2, deep, tile)
 
-    each(0, 4, incoming_tile)
+    each(0, 2, incoming_tile)
     reduce1.drain()
     each(0, RING, lambda pos: give1(pos).wait_send())
     shares[1].turn()
+    shares[0].partner()
     shares[1].own()
 
     def normalize_two(path):
@@ -479,6 +508,8 @@
     column[0][2].wait_recv()
     each(0, 2, slope_tile(0))
     shares[1].partner()
+    shares[0].finish()
+    each(2, 4, incoming_tile)
     shares[1].finish()
     normalize_two(1)
     each(0, 2, slope_tile(1))
@@ -622,20 +653,21 @@
     sums[0][2].start()
     plane[0].forward()
 
-    def along_back(step):
+    def along_back(step, m):
         other = wrap(col + step)
+        number = 16 + 4 * m + step
         return remote(
-            mid.at[other], final1.at[col], col_send.at[16 + step], col_recv.at[16 + step],
+            mid.at[m, other], final1.at[m, col], col_send.at[number], col_recv.at[number],
             (level, row * RING + other, core),
         )
 
     for m in (1, 0):
         plane[m].finish()
         for part in range(2):
-            mid[2 * part:2 * part + 2, m] = plane[m].total(part).astype(BF16)
-    for step in (2, 1, 3):
-        along_back(step).start()
-    final1[col] = mid[col]
+            mid[m, 2 * part:2 * part + 2] = plane[m].total(part).astype(BF16)
+        for step in (2, 1, 3):
+            along_back(step, m).start()
+        final1[m, col] = mid[m, col]
     own_side = pl.ds(pl.multiple_of(side * hidden2, hidden2), hidden2)
     other_side = pl.ds(pl.multiple_of((1 - side) * hidden2, hidden2), hidden2)
     for m in (1, 0):
@@ -643,10 +675,11 @@
         sum2[m, :, own_side] = (terms2[level, m].astype(F32) + near2[m].astype(F32)).astype(BF16)
         sums[m][2].wait_recv()
         sum2[m, :, other_side] = far2[m]
-    for step in (1, 3, 2):
-        along_back(step).wait_recv()
-    for q in range(RING):
-        sum1[:, :, q * hidden1:(q + 1) * hidden1] = final1[q]
+    for m in (1, 0):
+        for step in (1, 3, 2):
+            along_back(step, m).wait_recv()
+        for q in range(RING):
+            sum1[m, :, q * hidden1:(q + 1) * hidden1] = final1[m, q]
 
     for copy in spread + column[0] + column[1] + sums[0] + sums[1]:
         copy.wait_send()
@@ -655,7 +688,8 @@
     for step in range(RING):
         lift_pair(step).wait_send()
     for step in (1, 2, 3):
-        along_back(step).wait_send()
+        along_back(step, 0).wait_send()
+        along_back(step, 1).wait_send()
     give2(0).wait_send()
     give2(1).wait_send()
     to_partner.wait_send()
@@ -674,20 +708,6 @@
     slots = groups * SLOT
     count, lanes = slots * block, blocks * block
     hidden = wt1.shape[-1]
-    inside = lax.broadcasted_iota(jnp.int32, (blocks, block), 1) < doc_len[:, None]
-    masked = jnp.where(inside[:, :, None], cot, jnp.zeros_like(cot)).reshape(lanes, width)
-    targets = route[:, 0]
-    shared = targets[:, None] == targets[None, :]
-    before = lax.broadcasted_iota(jnp.int32, (blocks, blocks), 0) > lax.broadcasted_iota(
-        jnp.int32, (blocks, blocks), 1
-    )
-    rank = jnp.sum((shared & before).astype(jnp.int32), axis=1)
-    target_row = (targets * SLOT + rank)[:, None] * block + jnp.arange(block, dtype=jnp.int32)[None]
-    pick = (
-        lax.broadcasted_iota(jnp.int32, (count, lanes), 0) == target_row.reshape(1, lanes)
-    ).astype(BF16)
-    rows = docs.reshape(lanes, width)
-
     whole = pl.BlockSpec(memory_space=pltpu.VMEM)
     anywhere = pl.BlockSpec(memory_space=pl.ANY)
     half, quarter = width // 2, width // 4
@@ -708,9 +728,10 @@
             jax.ShapeDtypeStruct((2, small, hidden), BF16),
             jax.ShapeDtypeStruct((2, quarter, hidden), BF16),
         ),
-        in_specs=[whole, whole, whole, anywhere, anywhere],
+        in_specs=[whole, whole, whole, whole, anywhere, anywhere],
         out_specs=[whole, whole],
         scratch_shapes=[
+            vmem(count, lanes),
             vmem(2, small, hidden, kind=F32),
             vmem(2, 2, quarter, hidden2, kind=F32),
             vmem(RING, 2, small, hidden1),
@@ -746,8 +767,8 @@
             vmem(2, 2, 2, small, hidden1),
             vmem(2, 2, 2, small, hidden1),
             vmem(2, 4, 2, small, hidden1),
-            vmem(RING, 2, small, hidden1),
-            vmem(RING, 2, small, hidden1),
+            vmem(2, RING, small, hidden1),
+            vmem(2, RING, small, hidden1),
             dma(9, 6),
             dma(9, 6),
             dma(3, groups),
@@ -756,15 +777,15 @@
             dma(3, 2, groups),
             dma(14),
             dma(14),
-            dma(20),
-            dma(20),
+            dma(24),
+            dma(24),
             dma(5),
         ],
         compiler_params=pltpu.CompilerParams(
             collective_id=0, has_side_effects=True, vmem_limit_bytes=VMEM_LIMIT
         ),
         name="window",
-    )(rows, masked, pick, wt1[0], wt2[0])
+    )(docs.reshape(lanes, width), cot.reshape(lanes, width), route, doc_len[None], wt1[0], wt2[0])
 
     delta1 = sum1.astype(F32) / groups
     delta2 = sum2.astype(F32) / levels

time: 172 us -> 157 us (0.913)
  Pallas kernels: 156 us -> 145 us
  other arithmetic: 15.1 us -> 10 us
    pallas_call x1, Pallas kernels: 156 us -> 145 us  [local(): pl.pallas_call(kernel, out_shape=(jax.ShapeDtypeStruct((2, small, hidden)...]
    select_n x1 -> x0, other arithmetic: 1.94 us -> none  [local(): jnp.where(inside[:, :, None], cot, jnp.zeros_like(cot))]
where the time goes in v3:
time: 157 us
  Pallas kernels  145 us (92%)
  other arithmetic  10 us (6%)
    pallas_call x1, Pallas kernels, local(): pl.pallas_call(kernel, out_shape=(jax.ShapeDtypeStruct((2, small, hidden)...  145 us
    sub x2, other arithmetic, outer_step(): weights - OUTER_RATE * (delta[None] + MOMENTUM * new_moment)  10 us

profile of v3, /device:TPU:1, one launch (start us, length us, event | category | flops | bytes accessed | tf_op | source)
XLA Modules:
  0.0 156.9 jit_solution(18169598697816785933)
XLA Ops:
  0.6 1.3 copy.12.route
  2.0 0.0 copy-start
  2.0 144.8 %window.1 = (bf16[2,64,2048]{2,1,0:T(8,128)(2,1)}, bf16[2,256,2048]{2,1,0:T(8,128)(2,1)}) custom-call(bf16[256,1024]{1,0:T(8,128)(2,1)} %bitcast.23, bf16[256,1024]{1,0:T(8,128)(2,1)} %bitcast.24, s32[16,1]{1,0:T(8,128)} %copy.12.route, s32[1,16]{1,0:T(1,128)} %bitcast.25, f32[2,64,2048]{2,1,0:T(8,128)} %bitcast.22, f32[2,256,2048]{2,1,0:T(8,128)} %bitcast.21), custom_call_target="tpu_custom_call" | custom-call | tf_op jit(solution)/shard_map/window/pallas_call | solution.py:725
  146.8 0.0 copy-done
  146.8 0.0 copy-start.1
  146.8 0.0 copy-start.2
  146.8 0.0 copy-start.3
  146.8 8.4 %fusion.1 = (f32[1,2,256,2048]{3,2,1,0:T(8,128)}, f32[1,2,256,2048]{3,2,1,0:T(8,128)}) fusion(f32[1,2,256,2048]{3,2,1,0:T(8,128)S(1)} %copy-done, bf16[2,256,2048]{2,1,0:T(8,128)(2,1)} %get-tuple-element.7, f32[1,2,256,2048]{3,2,1,0:T(8,128)} %param.15), kind=kLoop, calls=%fused_computation.3 | loop fusion | flops 8388608 | bytes 18874368 | tf_op jit(solution)/shard_map/sub | solution.py:701
  155.2 0.0 copy-done.1
  155.2 0.0 copy-done.2
  155.3 0.0 copy-done.3
  155.3 1.6 %fusion.3 = (f32[1,2,64,2048]{3,2,1,0:T(8,128)}, f32[1,2,64,2048]{3,2,1,0:T(8,128)}) fusion(f32[1,2,64,2048]{3,2,1,0:T(8,128)S(1)} %copy-done.1, bf16[2,64,2048]{2,1,0:T(8,128)(2,1)S(1)} %copy-done.3, f32[1,2,64,2048]{3,2,1,0:T(8,128)S(1)} %copy-done.2), kind=kLoop, calls=%fused_computation.8 | loop fusion | flops 2097152 | bytes 4718592 | tf_op jit(solution)/shard_map/sub | solution.py:701
Async XLA Ops:
  2.0 144.8 %copy-start = (f32[1,2,256,2048]{3,2,1,0:T(8,128)S(1)}, f32[1,2,256,2048]{3,2,1,0:T(8,128)}, u32[]{:S(2)}) copy-start(f32[1,2,256,2048]{3,2,1,0:T(8,128)} %param.14) | copy-start | bytes 12582916
  146.8 8.5 %copy-start.1 = (f32[1,2,64,2048]{3,2,1,0:T(8,128)S(1)}, f32[1,2,64,2048]{3,2,1,0:T(8,128)}, u32[]{:S(2)}) copy-start(f32[1,2,64,2048]{3,2,1,0:T(8,128)} %param.12) | copy-start | bytes 3145732
  146.8 8.5 %copy-start.2 = (f32[1,2,64,2048]{3,2,1,0:T(8,128)S(1)}, f32[1,2,64,2048]{3,2,1,0:T(8,128)}, u32[]{:S(2)}) copy-start(f32[1,2,64,2048]{3,2,1,0:T(8,128)} %param.13) | copy-start | bytes 3145732
  146.8 8.5 %copy-start.3 = (bf16[2,64,2048]{2,1,0:T(8,128)(2,1)S(1)}, bf16[2,64,2048]{2,1,0:T(8,128)(2,1)}, u32[]{:S(2)}) copy-start(bf16[2,64,2048]{2,1,0:T(8,128)(2,1)} %get-tuple-element.6) | copy-start | bytes 1572868

commit v4 on v3

--- a/solution.py
+++ b/solution.py
@@ -14,7 +14,7 @@
 BF16 = jnp.bfloat16
 F32 = jnp.float32
 RING = 4
-VMEM_LIMIT = 57 * 1024 * 1024
+VMEM_LIMIT = 50 * 1024 * 1024
 
 
 def dot(left, right, contract=(1, 0)):
@@ -224,11 +224,11 @@
 
 def slot_matrix(route, pick):
     count, lanes = pick.shape
-    docs = route.shape[0]
+    docs = route.shape[1]
     block = lanes // docs
-    target = route[...].astype(F32)
-    spread = jnp.broadcast_to(target, (docs, 128))
-    by_row = dot(spread, doc_of_row(lanes, docs), (0, 1))[0:docs]
+    spread = jnp.broadcast_to(route[...].astype(F32), (128, docs))
+    by_row = dot(spread, doc_of_row(lanes, docs), (1, 1))[0:docs]
+    target = dot(doc_of_row(docs, docs), spread, (1, 1))[:, 0:1]
     own = lax.broadcasted_iota(jnp.int32, (docs, lanes), 1)
     earlier = lax.broadcasted_iota(jnp.int32, (docs, lanes), 0) < own // block
     rank = jnp.sum(jnp.where((by_row == target) & earlier, 1.0, 0.0), axis=0, keepdims=True)
@@ -251,12 +251,12 @@
 
 def kernel(
     docs, cot_docs, route, doc_len, wt1, wt2,
-    sum1, sum2,
-    pick,
-    stage1, stage2, own1, own2, weights1, weights2,
+    sum1, sum2_out,
+    pick, sum2,
+    stage1, stage2, own1, weights1, weights2,
     normed1, act1, gate1, part1, joined1, through1, summed1, landed1, out1,
     packed, cot, rows, back,
-    normed2, act2, slopes2, dn_sum, dn_far, mean_out, mean_in,
+    act2, slopes2, dn_sum, dn_far, mean_out, mean_in,
     terms2, near2, via2, far2,
     upstream, terms1, through_x, summed_x, landed_x, mid, final1,
     ring_send, ring_recv, swap_send, swap_recv, share_send, share_recv, pair_send, pair_recv,
@@ -300,28 +300,31 @@
             own1[q, m] = stage1[m, :, q * hidden1:(q + 1) * hidden1].astype(BF16)
     weights1[base] = own1[col]
 
-    def along(step):
+    def along(m, step):
         other = wrap(col + step)
+        number = 4 * m + step
         return remote(
-            own1.at[other],
-            weights1.at[base],
-            col_send.at[step],
-            col_recv.at[step],
+            own1.at[other, m],
+            weights1.at[base, m],
+            share_send.at[2, 1, number],
+            share_recv.at[2, 1, number],
             (level, row * RING + other, core),
         )
 
-    def gather_x(step, number):
+    def gather_x(m, step, number):
         fixed = wrap(col + step)
-        land = lambda pos, m: weights1.at[pos * RING + fixed, m]
-        own = (lambda m: own1.at[col, m]) if step == 0 else (lambda m: land(row, m))
+        rows_of = lambda part: pl.ds(part * (block // 2), block // 2)
+        land = lambda pos, part: weights1.at[pos * RING + fixed, m, rows_of(part)]
+        own = (lambda part: own1.at[col, m, rows_of(part)]) if step == 0 else (lambda part: land(row, part))
         device = lambda pos: (level, pos * RING + col, core)
         return Gather(own, land, row, device, ring_send.at[number], ring_recv.at[number])
 
-    spread = [along(step) for step in (1, 3, 2)]
-    gathers = [gather_x(step, k) for k, step in enumerate((0, 3, 1, 2))]
-    for copy in spread:
-        copy.start()
-    gathers[0].start()
+    spread = [[along(m, step) for step in (1, 3, 2)] for m in range(2)]
+    gathers = [[gather_x(m, step, 4 * m + k) for k, step in enumerate((0, 3, 1, 2))] for m in range(2)]
+    for m in range(2):
+        for copy in spread[m]:
+            copy.start()
+        gathers[m][0].start()
 
     rows_half = lanes // 2
     rows_part = rows_half // 2
@@ -335,8 +338,8 @@
         doc_part,
         col,
         on_y,
-        ring_send.at[4],
-        ring_recv.at[4],
+        ring_send.at[8],
+        ring_recv.at[8],
     )
     def doc_pair(step):
         where = normed1.at[wrap(col + step), pl.ds(pl.multiple_of(core * rows_half, rows_half), rows_half)]
@@ -344,8 +347,8 @@
 
     def down_z(m):
         return [
-            remote(own2.at[1 - side, m], weights2.at[level, m], col_send.at[4 + m], col_recv.at[4 + m], partner_chip),
-            remote(own2.at[side, m], weights2.at[level, m], col_send.at[6 + m], col_recv.at[6 + m], mate_chip),
+            remote(act2.at[1 - side, m], weights2.at[level, m], col_send.at[4 + m], col_recv.at[4 + m], partner_chip),
+            remote(act2.at[side, m], weights2.at[level, m], col_send.at[6 + m], col_recv.at[6 + m], mate_chip),
             remote(weights2.at[partner, m], weights2.at[partner, m], col_send.at[8 + m], col_recv.at[8 + m], mate_chip),
         ]
 
@@ -353,10 +356,10 @@
     for m in (1, 0):
         for h in range(2):
             loads[1 + 2 * m + h].wait()
-            own2[h, m] = stage2[h, m].astype(BF16)
+            act2[h, m] = stage2[h, m].astype(BF16)
         column[m][0].start()
         column[m][1].start()
-        weights2[level, m] = own2[side, m]
+        weights2[level, m] = act2[side, m]
 
     left = pl.ds(pl.multiple_of(core * half, half), half)
     swaps = [
@@ -375,15 +378,18 @@
     masked = jnp.where(live, cot_docs[:, left], jnp.zeros((lanes, half), BF16))
     packed[...] = dot(pick[...], masked).astype(BF16).reshape(packed.shape)
 
-    for k, copy in enumerate((spread[0], spread[1], spread[2])):
-        copy.wait_recv()
-        gathers[1 + k].start()
-    documents.start()
-    for gather in gathers[:3]:
-        gather.forward()
-    column[1][0].wait_recv()
-    column[1][2].start()
-    gathers[3].forward()
+    for m in range(2):
+        for k, copy in enumerate(spread[m]):
+            copy.wait_recv()
+            gathers[m][1 + k].start()
+        if m == 0:
+            documents.start()
+        for gather in gathers[m][:3]:
+            gather.forward()
+        if m == 1:
+            column[1][0].wait_recv()
+            column[1][2].start()
+        gathers[m][3].forward()
     documents.forward()
     documents.near()
     doc_pair(3).start()
@@ -401,52 +407,68 @@
         normed1[number] = (floated * rms_of(square, width)).astype(BF16)
 
     each(0, RING, normalize_one)
-    for gather in gathers:
+    for gather in gathers[0]:
         gather.near()
         gather.far()
-    swaps[0].start()
 
     def matrix1(m):
         return weights1[:, m].reshape(width, hidden1)
 
-    def give1(pos):
+    def give1(step):
+        pos = wrap(col + step)
         return remote(
-            part1.at[pos, 1 - core], joined1.at[pos], share_send.at[2, 0, pos], share_recv.at[2, 0, pos], sibling
-        )
-
-    def level_one(number):
-        pos = lax.rem(col + 2 + 3 * number, RING)
+            part1.at[pos, 1 - core], joined1.at[pos], share_send.at[2, 0, step], share_recv.at[2, 0, step], sibling
+        )
+
+    def up_one(pos):
         pre = dot(normed1[pos], matrix1(0))
         sigma = jax.nn.sigmoid(pre)
-        active = (pre * sigma).astype(BF16)
-        act1[pos] = active
+        act1[pos] = (pre * sigma).astype(BF16)
         gate1[pos] = (sigma * (1.0 + pre * (1.0 - sigma))).astype(BF16)
-        for h in range(2):
-            piece = weights1[8 * h:8 * h + 8, 1].reshape(half, hidden1)
-            part1[pos, h] = dot(active, piece, (1, 1)).astype(BF16)
-        give1(pos).start()
-
-    each(0, RING, level_one)
-
-    def join_one(number):
-        pos = lax.rem(col + 2 + 3 * number, RING)
-        give1(pos).wait_recv()
+
+    def down_one(step):
+        pos = wrap(col + step)
+        for number in range(2):
+            h = lax.rem(1 - core + number, 2)
+            piece = weights1[pl.ds(8 * h, 8), 1].reshape(half, hidden1)
+            part1[pos, h] = dot(act1[pos], piece, (1, 1)).astype(BF16)
+            if number == 0:
+                give1(step).start()
+
+    def join_one(step):
+        pos = wrap(col + step)
+        give1(step).wait_recv()
         joined1[pos] = (part1[pos, core].astype(F32) + joined1[pos].astype(F32)).astype(BF16)
 
-    each(0, RING, join_one)
+    each(0, RING, up_one)
+    for gather in gathers[1]:
+        gather.near()
+        gather.far()
     hold = lanes // 2
     reduce1 = Scatter(
         lambda pos, part: joined1.at[pos, pl.ds(part * hold, hold)],
         (through1, summed1, landed1),
         col,
         on_y,
-        ring_send.at[5],
-        ring_recv.at[5],
+        ring_send.at[9],
+        ring_recv.at[9],
     )
-    reduce1.start()
+    down_one(2)
+    down_one(1)
+    join_one(2)
+    reduce1.first[0].start()
+    reduce1.first[1].start()
+    down_one(3)
+    join_one(1)
+    reduce1.first[2].start()
+    down_one(0)
+    join_one(3)
+    reduce1.first[3].start()
+    swaps[0].start()
     column[0][0].wait_recv()
     column[0][2].start()
     reduce1.forward()
+    join_one(0)
     shares[0].turn()
     reduce1.finish()
     for part in range(2):
@@ -478,7 +500,8 @@
 
     each(0, 2, incoming_tile)
     reduce1.drain()
-    each(0, RING, lambda pos: give1(pos).wait_send())
+    for step in range(RING):
+        give1(step).wait_send()
     shares[1].turn()
     shares[0].partner()
     shares[1].own()
@@ -489,65 +512,85 @@
         )
         factor = rms_of(square, width)
         for h in range(2):
-            normed2[path, h] = (flat(rows, path, h).astype(F32) * factor).astype(BF16)
+            value = (flat(rows, path, h).astype(F32) * factor).astype(BF16)
+            terms1[2 * path:2 * path + 2, h] = value.reshape(2, RING, block, half)
         return factor
 
-    def slope_tile(path):
+    def normed2(path, h):
+        return terms1[2 * path:2 * path + 2, h].reshape(count, half)
+
+    def slope_tile(path, first, parts):
+        where = slice(first, first + parts)
+
         def step(number):
             columns = columns_of(number)
-            pre = dot(normed2[path, 0], piece2(0, 0, columns)) + dot(normed2[path, 1], piece2(0, 1, columns))
+            lefts = [
+                terms1[2 * path + first:2 * path + first + parts, h].reshape(parts * deep, half) for h in range(2)
+            ]
+            pre = dot(lefts[0], piece2(0, 0, columns)) + dot(lefts[1], piece2(0, 1, columns))
             sigma = jax.nn.sigmoid(pre)
-            incoming = stage2[path, :, :, columns].reshape(count, tile)
-            act2[path, :, columns] = (pre * sigma).astype(BF16)
-            slopes2[path, :, columns] = (incoming * sigma * (1.0 + pre * (1.0 - sigma))).astype(BF16)
+            incoming = stage2[path, where, :, columns].reshape(parts * deep, tile)
+            slope = (incoming * sigma * (1.0 + pre * (1.0 - sigma))).astype(BF16)
+            act2[path, where, :, columns] = (pre * sigma).astype(BF16).reshape(parts, deep, tile)
+            slopes2[path, where, :, columns] = slope.reshape(parts, deep, tile)
 
         return step
 
     factor = normalize_two(0)
     column[0][1].wait_recv()
     column[0][2].wait_recv()
-    each(0, 2, slope_tile(0))
+    for m in range(2):
+        column[m][0].wait_send()
+        column[m][1].wait_send()
+    each(0, 2, slope_tile(0, 0, 2))
     shares[1].partner()
     shares[0].finish()
     each(2, 4, incoming_tile)
     shares[1].finish()
     normalize_two(1)
-    each(0, 2, slope_tile(1))
-
-    def give2(path):
-        where = pl.ds(2 * path, 2)
+
+    def give2(spot):
         return remote(
-            part1.at[where, 1 - core], joined1.at[where], pair_send.at[6 + path], pair_recv.at[6 + path], sibling
-        )
-
-    def dn_tiles(path):
-        def step(number):
+            part1.at[spot, 1 - core], joined1.at[spot], share_send.at[2, 0, 4 + spot], share_recv.at[2, 0, 4 + spot], sibling
+        )
+
+    def dn_tiles(path, first, parts):
+        for number in range(2):
             h = lax.rem(1 - core + number, 2)
             piece = weights2[pl.ds(2 * h, 2), 0].reshape(half, hidden2)
-            value = dot(slopes2[path], piece, (1, 1)).astype(BF16)
-            part1[2 * path:2 * path + 2, h] = value.reshape(2, lanes, half)
-
-        each(0, 1, step)
-        give2(path).start()
-        each(1, 2, step)
-
-    def dn_of(path):
-        where = slice(2 * path, 2 * path + 2)
-        return (part1[where, core].astype(F32) + joined1[where].astype(F32)).reshape(count, half)
-
-    to_partner = remote(dn_sum, dn_far, pair_send.at[8], pair_recv.at[8], partner_chip)
-    dn_tiles(1)
-    give2(1).wait_recv()
-    dn_sum[...] = dn_of(1).astype(BF16)
-    to_partner.start()
-    dn_tiles(0)
+            left2 = slopes2[path, first:first + parts].reshape(parts * deep, hidden2)
+            value = dot(left2, piece, (1, 1)).astype(BF16)
+            part1[2 * path + first:2 * path + first + parts, h] = value.reshape(parts, deep, half)
+            if number == 0:
+                for spot in range(2 * path + first, 2 * path + first + parts):
+                    give2(spot).start()
+
+    def dn_of(spot):
+        return part1[spot, core].astype(F32) + joined1[spot].astype(F32)
+
+    def to_partner(part):
+        return remote(dn_sum.at[part], dn_far.at[part], pair_send.at[6 + part], pair_recv.at[6 + part], partner_chip)
+
+    def dn_out(part):
+        give2(2 + part).wait_recv()
+        dn_sum[part] = dn_of(2 + part).astype(BF16)
+        to_partner(part).start()
+
+    each(0, 2, slope_tile(1, 0, 1))
+    dn_tiles(1, 0, 1)
+    each(0, 2, slope_tile(1, 1, 1))
+    dn_out(0)
+    dn_tiles(1, 1, 1)
+    dn_out(1)
+    dn_tiles(0, 0, 2)
 
     def term_tiles(m, lefts, right):
         def step(number):
             columns = columns_of(number)
             for h in range(2):
-                value = dot(lefts(0, h), right[0, :, columns], (0, 0)) + dot(
-                    lefts(1, h), right[1, :, columns], (0, 0)
+                value = sum(
+                    dot(lefts(path, h), right[path, :, :, columns].reshape(count, tile), (0, 0))
+                    for path in range(2)
                 )
                 terms2[2 * h:2 * h + 2, m, :, columns] = value.astype(BF16).reshape(2, deep, tile)
 
@@ -565,11 +608,13 @@
     sums[1][0].start()
     sums[1][1].start()
 
-    give2(0).wait_recv()
-    to_partner.wait_recv()
+    for part in range(2):
+        give2(part).wait_recv()
+        to_partner(part).wait_recv()
 
     def pieces():
-        return flat(rows, 0, core).astype(F32) * factor, dn_of(0) + dn_far[...].astype(F32)
+        value = jnp.concatenate([dn_of(part) + dn_far[part].astype(F32) for part in range(2)], axis=0)
+        return flat(rows, 0, core).astype(F32) * factor, value
 
     normed, value = pieces()
     mean = jnp.sum(value * normed, axis=-1, keepdims=True)
@@ -583,7 +628,7 @@
     swaps[1].drain()
     packed[...] = result.astype(BF16).reshape(packed.shape)
     swaps[2].start()
-    term_tiles(0, lambda path, h: normed2[path, h], slopes2)
+    term_tiles(0, normed2, slopes2)
     sums[0][0].start()
     sums[0][1].start()
     sums[1][0].wait_recv()
@@ -597,8 +642,8 @@
         lambda pos, part: upstream.at[pos, core, pl.ds(part * hold, hold)],
         col,
         on_y,
-        ring_send.at[6],
-        ring_recv.at[6],
+        ring_send.at[10],
+        ring_recv.at[10],
     )
     lifts.start()
 
@@ -612,20 +657,16 @@
     lift_pair(3).start()
     lift_pair(1).start()
 
-    def slope_one(step):
-        pos = wrap(col + step)
-        lift_pair(step).wait_recv()
+    def slope_one(pos):
         incoming = dot(upstream[pos, 0], weights1[0:8, 1].reshape(half, hidden1)) + dot(
             upstream[pos, 1], weights1[8:16, 1].reshape(half, hidden1)
         )
         joined1[pos] = (incoming * gate1[pos].astype(F32)).astype(BF16)
 
-    slope_one(0)
     lifts.far()
     lift_pair(2).start()
-    slope_one(3)
-    slope_one(1)
-    slope_one(2)
+    for step in range(RING):
+        lift_pair(step).wait_recv()
 
     def term_one(m, lefts, right):
         for h in range(2):
@@ -638,13 +679,14 @@
             (through_x.at[m], summed_x.at[m], landed_x.at[m]),
             row,
             lambda pos: (level, pos * RING + col, core),
-            ring_send.at[7 + m],
-            ring_recv.at[7 + m],
+            ring_send.at[11 + m],
+            ring_recv.at[11 + m],
         )
 
     plane = [scatter_x(m) for m in range(2)]
     term_one(1, lambda h: upstream[:, h], act1)
     plane[1].start()
+    each(0, RING, slope_one)
     term_one(0, lambda h: normed1[:, :, h * half:(h + 1) * half], joined1)
     plane[0].start()
     plane[1].forward()
@@ -675,25 +717,29 @@
         sum2[m, :, own_side] = (terms2[level, m].astype(F32) + near2[m].astype(F32)).astype(BF16)
         sums[m][2].wait_recv()
         sum2[m, :, other_side] = far2[m]
+    keep = pltpu.make_async_copy(sum2, sum2_out, local_sem.at[0])
+    keep.start()
     for m in (1, 0):
         for step in (1, 3, 2):
             along_back(step, m).wait_recv()
         for q in range(RING):
             sum1[m, :, q * hidden1:(q + 1) * hidden1] = final1[m, q]
 
-    for copy in spread + column[0] + column[1] + sums[0] + sums[1]:
+    for copy in spread[0] + spread[1] + [column[0][2], column[1][2]] + sums[0] + sums[1]:
         copy.wait_send()
-    for ring in gathers + [lifts] + plane + [swaps[2]] + shares:
+    for ring in gathers[0] + gathers[1] + [lifts] + plane + [swaps[2]] + shares:
         ring.drain()
     for step in range(RING):
         lift_pair(step).wait_send()
     for step in (1, 2, 3):
         along_back(step, 0).wait_send()
         along_back(step, 1).wait_send()
+        give2(step).wait_send()
     give2(0).wait_send()
-    give2(1).wait_send()
-    to_partner.wait_send()
+    to_partner(0).wait_send()
+    to_partner(1).wait_send()
     swap_mean.wait_send()
+    keep.wait()
 
 
 def outer_step(weights, moment, delta):
@@ -729,13 +775,13 @@
             jax.ShapeDtypeStruct((2, quarter, hidden), BF16),
         ),
         in_specs=[whole, whole, whole, whole, anywhere, anywhere],
-        out_specs=[whole, whole],
+        out_specs=[whole, anywhere],
         scratch_shapes=[
             vmem(count, lanes),
+            vmem(2, quarter, hidden),
             vmem(2, small, hidden, kind=F32),
             vmem(2, 2, quarter, hidden2, kind=F32),
             vmem(RING, 2, small, hidden1),
-            vmem(2, 2, quarter, hidden2),
             vmem(16, 2, small, hidden1),
             vmem(RING, 2, quarter, hidden2),
             vmem(RING, lanes, width),
@@ -751,11 +797,10 @@
             vmem(2, 2, groups, per, half),
             vmem(2, 2, groups, per, half),
             vmem(groups, per, half),
-            vmem(2, 2, count, half),
-            vmem(2, count, hidden2),
-            vmem(2, count, hidden2),
-            vmem(count, half),
-            vmem(count, half),
+            vmem(2, 2, quarter, hidden2),
+            vmem(2, 2, quarter, hidden2),
+            vmem(2, quarter, half),
+            vmem(2, quarter, half),
             vmem(count, 128, kind=F32),
             vmem(count, 128, kind=F32),
             vmem(RING, 2, quarter, hidden2),
@@ -769,8 +814,8 @@
             vmem(2, 4, 2, small, hidden1),
             vmem(2, RING, small, hidden1),
             vmem(2, RING, small, hidden1),
-            dma(9, 6),
-            dma(9, 6),
+            dma(13, 6),
+            dma(13, 6),
             dma(3, groups),
             dma(3, groups),
             dma(3, 2, groups),
@@ -785,7 +830,7 @@
             collective_id=0, has_side_effects=True, vmem_limit_bytes=VMEM_LIMIT
         ),
         name="window",
-    )(docs.reshape(lanes, width), cot.reshape(lanes, width), route, doc_len[None], wt1[0], wt2[0])
+    )(docs.reshape(lanes, width), cot.reshape(lanes, width), route.T, doc_len[None], wt1[0], wt2[0])
 
     delta1 = sum1.astype(F32) / groups
     delta2 = sum2.astype(F32) / levels

time: 157 us -> 162 us (1.032)
  local copies, waits for them, and re-layouts: 1.35 us -> 4.62 us
  Pallas kernels: 145 us -> 147 us
    unnamed x9 -> x14, local copies, waits for them, and re-layouts: 1.35 us -> 4.62 us
    pallas_call x1, Pallas kernels: 145 us -> 147 us  [local(): pl.pallas_call(kernel, out_shape=(jax.ShapeDtypeStruct((2, small, hidden)...]
where the time goes in v4:
time: 162 us; the launch traced here: 161 us
  Pallas kernels  147 us (91%)
  other arithmetic  9.49 us (6%)
  local copies, waits for them, and re-layouts  4.62 us (3%)
    pallas_call x1, Pallas kernels, local(): pl.pallas_call(kernel, out_shape=(jax.ShapeDtypeStruct((2, small, hidden)...  147 us
    sub x2, other arithmetic, outer_step(): weights - OUTER_RATE * (delta[None] + MOMENTUM * new_moment)  9.49 us
    unnamed x14, local copies, waits for them, and re-layouts  4.62 us

profile of v4, /device:TPU:1, one launch (start us, length us, event | category | flops | bytes accessed | tf_op | source)
XLA Modules:
  0.0 161.5 jit_solution(3457540349908209716)
XLA Ops:
  0.6 0.0 copy-start
  0.6 1.2 copy-done
  1.9 0.0 copy-start.1
  1.9 1.0 copy-done.1
  2.9 0.0 copy-start.2
  2.9 1.0 copy-done.2
  3.9 0.0 copy-start.3
  3.9 0.7 copy-done.3
  4.6 0.0 copy-start.4
  4.6 0.7 copy-done.4
  5.3 0.0 copy-start.5
  5.3 146.7 %window.1 = (bf16[2,64,2048]{2,1,0:T(8,128)(2,1)S(1)}, bf16[2,256,2048]{2,1,0:T(8,128)(2,1)}) custom-call(bf16[256,1024]{1,0:T(8,128)(2,1)S(1)} %bitcast.23, bf16[256,1024]{1,0:T(8,128)(2,1)S(1)} %bitcast.24, s32[1,16]{1,0:T(1,128)S(1)} %bitcast.25, s32[1,16]{1,0:T(1,128)S(1)} %bitcast.26, f32[2,64,2048]{2,1,0:T(8,128)S(1)} %bitcast.22, f32[2,256,2048]{2,1,0:T(8,128)} %bitcast.27), custom_call_target="tpu_custom_call" | custom-call | tf_op jit(solution)/shard_map/window/pallas_call | solution.py:771
  152.0 0.0 copy-done.5
  152.0 0.0 copy-start.6
  152.0 7.9 %fusion.1 = (f32[1,2,256,2048]{3,2,1,0:T(8,128)}, f32[1,2,256,2048]{3,2,1,0:T(8,128)}) fusion(f32[1,2,256,2048]{3,2,1,0:T(8,128)S(1)} %copy-done.5, bf16[2,256,2048]{2,1,0:T(8,128)(2,1)} %get-tuple-element.7, f32[1,2,256,2048]{3,2,1,0:T(8,128)} %param.15), kind=kLoop, calls=%fused_computation.3 | loop fusion | flops 8388608 | bytes 18874368 | tf_op jit(solution)/shard_map/sub | solution.py:747
  159.8 0.0 copy-done.6
  159.9 1.6 fusion.3
Async XLA Ops:
  0.6 1.2 copy-start
  1.9 1.0 copy-start.1
  2.9 1.0 copy-start.2
  3.9 0.7 copy-start.3
  4.6 0.7 copy-start.4
  5.3 146.7 %copy-start.5 = (f32[1,2,256,2048]{3,2,1,0:T(8,128)S(1)}, f32[1,2,256,2048]{3,2,1,0:T(8,128)}, u32[]{:S(2)}) copy-start(f32[1,2,256,2048]{3,2,1,0:T(8,128)} %param.14) | copy-start | bytes 12582916
  152.0 7.9 %copy-start.6 = (f32[1,2,64,2048]{3,2,1,0:T(8,128)S(1)}, f32[1,2,64,2048]{3,2,1,0:T(8,128)}, u32[]{:S(2)}) copy-start(f32[1,2,64,2048]{3,2,1,0:T(8,128)} %param.13) | copy-start | bytes 3145732

commit v5 on v4

--- a/solution.py
+++ b/solution.py
@@ -1,3 +1,5 @@
+import functools
+
 import jax
 import jax.numpy as jnp
 from jax import lax
@@ -14,7 +16,7 @@
 BF16 = jnp.bfloat16
 F32 = jnp.float32
 RING = 4
-VMEM_LIMIT = 50 * 1024 * 1024
+VMEM_LIMIT = 57 * 1024 * 1024
 
 
 def dot(left, right, contract=(1, 0)):
@@ -396,6 +398,7 @@
     doc_pair(1).start()
     documents.far()
     doc_pair(2).start()
+    swaps[0].start()
     normed1[col] = docs[...]
     documents.drain()
     for step in (1, 2, 3):
@@ -464,7 +467,6 @@
     down_one(0)
     join_one(3)
     reduce1.first[3].start()
-    swaps[0].start()
     column[0][0].wait_recv()
     column[0][2].start()
     reduce1.forward()
@@ -742,9 +744,18 @@
     keep.wait()
 
 
-def outer_step(weights, moment, delta):
-    new_moment = MOMENTUM * moment + delta[None]
-    return (weights - OUTER_RATE * (delta[None] + MOMENTUM * new_moment), new_moment)
+def outer_step(scales, wt1, mom1, sum1, wt2, mom2, sum2, new_wt1, new_mom1, new_wt2, new_mom2):
+    def step(scale, weights, moment, total, new_weights, new_moment):
+        delta = total[...].astype(F32) / scale
+        moved = MOMENTUM * moment[...] + delta
+        new_moment[...] = moved
+        new_weights[...] = weights[...] - OUTER_RATE * (delta + MOMENTUM * moved)
+
+    step(scales[1], wt2, mom2, sum2, new_wt2, new_mom2)
+
+    @pl.when(pl.program_id(0) == 0)
+    def _():
+        step(scales[0], wt1, mom1, sum1, new_wt1, new_mom1)
 
 
 def local(docs, cot, route, doc_len, wt1, mom1, wt2, mom2):
@@ -832,11 +843,29 @@
         name="window",
     )(docs.reshape(lanes, width), cot.reshape(lanes, width), route.T, doc_len[None], wt1[0], wt2[0])
 
-    delta1 = sum1.astype(F32) / groups
-    delta2 = sum2.astype(F32) / levels
-    new_wt1, new_mom1 = outer_step(wt1, mom1, delta1)
-    new_wt2, new_mom2 = outer_step(wt2, mom2, delta2)
-    return (new_wt1, new_mom1, new_wt2, new_mom2)
+    flat1, flat2 = (2 * small, hidden), (2 * quarter, hidden)
+    steps = 4
+    once = pl.BlockSpec(flat1, lambda number: (0, 0))
+    part = pl.BlockSpec((flat2[0] // steps, hidden), lambda number: (number, 0))
+    results = pl.pallas_call(
+        functools.partial(outer_step, (groups, levels)),
+        grid=(steps,),
+        out_shape=[jax.ShapeDtypeStruct(flat, F32) for flat in (flat1, flat1, flat2, flat2)],
+        in_specs=[once] * 3 + [part] * 3,
+        out_specs=[once] * 2 + [part] * 2,
+        compiler_params=pltpu.CompilerParams(vmem_limit_bytes=VMEM_LIMIT),
+        name="outer",
+    )(
+        wt1.reshape(flat1),
+        mom1.reshape(flat1),
+        sum1.reshape(flat1),
+        wt2.reshape(flat2),
+        mom2.reshape(flat2),
+        sum2.reshape(flat2),
+    )
+    return tuple(
+        result.reshape(like.shape) for result, like in zip(results, (wt1, mom1, wt2, mom2))
+    )
 
 
 def solution(mesh):

time: 162 us -> 154 us (0.951)
  other arithmetic: 9.49 us -> 0 us
  Pallas kernels: 147 us -> 154 us
  local copies, waits for them, and re-layouts: 4.62 us -> 0 us
    pallas_call x0 -> x1, Pallas kernels: none -> 9.99 us  [local(): pl.pallas_call(functools.partial(outer_step, (groups, levels)), grid=(ste...]
    sub x2 -> x0, other arithmetic: 9.49 us -> none  [outer_step(): weights - OUTER_RATE * (delta[None] + MOMENTUM * new_moment)]
    unnamed x14 -> x0, local copies, waits for them, and re-layouts: 4.62 us -> none
    pallas_call x1, Pallas kernels: 147 us -> 144 us  [local(): pl.pallas_call(kernel, out_shape=(jax.ShapeDtypeStruct((2, small, hidden)...]
where the time goes in v5:
time: 154 us
  Pallas kernels  154 us (100%)
    pallas_call x1, Pallas kernels, local(): pl.pallas_call(kernel, out_shape=(jax.ShapeDtypeStruct((2, small, hidden)...  144 us
    pallas_call x1, Pallas kernels, local(): pl.pallas_call(functools.partial(outer_step, (groups, levels)), grid=(ste...  9.99 us

profile of v5, /device:TPU:1, one launch (start us, length us, event | category | flops | bytes accessed | tf_op | source)
XLA Modules:
  0.0 154.3 jit_solution(2662041774610184796)
XLA Ops:
  0.6 143.7 %window.1 = (bf16[2,64,2048]{2,1,0:T(8,128)(2,1)}, bf16[2,256,2048]{2,1,0:T(8,128)(2,1)}) custom-call(bf16[256,1024]{1,0:T(8,128)(2,1)} %bitcast.24, bf16[256,1024]{1,0:T(8,128)(2,1)} %bitcast.25, s32[1,16]{1,0:T(1,128)} %bitcast.26, s32[1,16]{1,0:T(1,128)} %bitcast.27, f32[2,64,2048]{2,1,0:T(8,128)} %bitcast.19, f32[2,256,2048]{2,1,0:T(8,128)} %bitcast.16), custom_call_target="tpu_custom_call" | custom-call | tf_op jit(solution)/shard_map/window/pallas_call | solution.py:782
  144.3 10.0 %outer.1 = (f32[128,2048]{1,0:T(8,128)}, f32[128,2048]{1,0:T(8,128)}, f32[512,2048]{1,0:T(8,128)}, f32[512,2048]{1,0:T(8,128)}) custom-call(f32[128,2048]{1,0:T(8,128)} %bitcast.20, f32[128,2048]{1,0:T(8,128)} %bitcast.22, bf16[128,2048]{1,0:T(8,128)(2,1)} %bitcast.23, f32[512,2048]{1,0:T(8,128)} %bitcast.17, f32[512,2048]{1,0:T(8,128)} %bitcast.18, ...), custom_call_target="tpu_custom_call" | custom-call | tf_op jit(solution)/shard_map/outer/pallas_call | solution.py:850

commit v6 on v5

--- a/solution.py
+++ b/solution.py
@@ -16,7 +16,7 @@
 BF16 = jnp.bfloat16
 F32 = jnp.float32
 RING = 4
-VMEM_LIMIT = 57 * 1024 * 1024
+VMEM_LIMIT = 54 * 1024 * 1024
 
 
 def dot(left, right, contract=(1, 0)):
@@ -392,13 +392,13 @@
             column[1][0].wait_recv()
             column[1][2].start()
         gathers[m][3].forward()
+    swaps[0].start()
     documents.forward()
     documents.near()
     doc_pair(3).start()
     doc_pair(1).start()
     documents.far()
     doc_pair(2).start()
-    swaps[0].start()
     normed1[col] = docs[...]
     documents.drain()
     for step in (1, 2, 3):
@@ -444,6 +444,7 @@
         joined1[pos] = (part1[pos, core].astype(F32) + joined1[pos].astype(F32)).astype(BF16)
 
     each(0, RING, up_one)
+    shares[0].turn()
     for gather in gathers[1]:
         gather.near()
         gather.far()
@@ -471,7 +472,6 @@
     column[0][2].start()
     reduce1.forward()
     join_one(0)
-    shares[0].turn()
     reduce1.finish()
     for part in range(2):
         where = slice(part * hold, (part + 1) * hold)
@@ -840,6 +840,7 @@
         compiler_params=pltpu.CompilerParams(
             collective_id=0, has_side_effects=True, vmem_limit_bytes=VMEM_LIMIT
         ),
+        cost_estimate=pl.CostEstimate(flops=100_000_000_000, bytes_accessed=40_000_000, transcendentals=2_000_000),
         name="window",
     )(docs.reshape(lanes, width), cot.reshape(lanes, width), route.T, doc_len[None], wt1[0], wt2[0])
 
@@ -853,7 +854,7 @@
         out_shape=[jax.ShapeDtypeStruct(flat, F32) for flat in (flat1, flat1, flat2, flat2)],
         in_specs=[once] * 3 + [part] * 3,
         out_specs=[once] * 2 + [part] * 2,
-        compiler_params=pltpu.CompilerParams(vmem_limit_bytes=VMEM_LIMIT),
+        compiler_params=pltpu.CompilerParams(vmem_limit_bytes=24 * 1024 * 1024),
         name="outer",
     )(
         wt1.reshape(flat1),

time: 154 us -> 154 us (level)
  Pallas kernels: 154 us -> 149 us
  local copies, waits for them, and re-layouts: 0 us -> 3.86 us
    pallas_call x1, Pallas kernels: 9.99 us -> 5.06 us  [local(): pl.pallas_call(functools.partial(outer_step, (groups, levels)), grid=(ste...]
    unnamed x0 -> x12, local copies, waits for them, and re-layouts: none -> 3.86 us
where the time goes in v6:
time: 154 us
  Pallas kernels  149 us (97%)
  local copies, waits for them, and re-layouts  3.86 us (3%)
    pallas_call x1, Pallas kernels, local(): pl.pallas_call(kernel, out_shape=(jax.ShapeDtypeStruct((2, small, hidden)...  144 us
    pallas_call x1, Pallas kernels, local(): pl.pallas_call(functools.partial(outer_step, (groups, levels)), grid=(ste...  5.06 us
    unnamed x12, local copies, waits for them, and re-layouts  3.86 us

profile of v6, /device:TPU:1, one launch (start us, length us, event | category | flops | bytes accessed | tf_op | source)
XLA Modules:
  0.0 153.9 jit_solution(6550914728579500746)
XLA Ops:
  0.6 0.0 copy-start
  0.6 0.0 copy-start.1
  0.7 0.0 copy-start.3
  0.7 144.3 %window.1 = (bf16[2,64,2048]{2,1,0:T(8,128)(2,1)}, bf16[2,256,2048]{2,1,0:T(8,128)(2,1)}) custom-call(bf16[256,1024]{1,0:T(8,128)(2,1)} %bitcast.28, bf16[256,1024]{1,0:T(8,128)(2,1)} %bitcast.29, s32[1,16]{1,0:T(1,128)} %bitcast.30, s32[1,16]{1,0:T(1,128)} %bitcast.31, f32[2,64,2048]{2,1,0:T(8,128)} %bitcast.20, f32[2,256,2048]{2,1,0:T(8,128)} %bitcast.16), custom_call_target="tpu_custom_call" | custom-call | flops 99999997952 | bytes 40000000 | tf_op jit(solution)/shard_map/window/pallas_call | solution.py:782
  144.9 0.0 copy-done
  145.0 0.0 copy-done.1
  145.0 0.0 copy-done.3
  145.0 0.0 copy-start.2
  145.0 1.6 %copy-done.2 = bf16[2,256,2048]{2,1,0:T(8,128)(2,1)S(1)} copy-done((bf16[2,256,2048]{2,1,0:T(8,128)(2,1)S(1)}, bf16[2,256,2048]{2,1,0:T(8,128)(2,1)}, u32[]{:S(2)}) %copy-start.2) | copy-done | bytes 2097176
  146.6 0.0 copy-start.4
  146.6 1.2 copy-done.4
  147.8 0.0 copy-start.5
  147.8 1.0 copy-done.5
  148.8 5.1 %outer.1 = (f32[128,2048]{1,0:T(8,128)}, f32[128,2048]{1,0:T(8,128)}, f32[512,2048]{1,0:T(8,128)}, f32[512,2048]{1,0:T(8,128)}) custom-call(f32[128,2048]{1,0:T(8,128)S(1)} %bitcast.21, f32[128,2048]{1,0:T(8,128)S(1)} %bitcast.22, bf16[128,2048]{1,0:T(8,128)(2,1)S(1)} %bitcast.23, f32[512,2048]{1,0:T(8,128)S(1)} %bitcast.17, f32[512,2048]{1,0:T(8,128)S(1)} %bitcast.18, ...), custom_call_target="tpu_custom_call" | custom-call | tf_op jit(solution)/shard_map/outer/pallas_call | solution.py:851
Async XLA Ops:
  0.6 144.3 %copy-start = (f32[1,2,256,2048]{3,2,1,0:T(8,128)S(1)}, f32[1,2,256,2048]{3,2,1,0:T(8,128)}, u32[]{:S(2)}) copy-start(f32[1,2,256,2048]{3,2,1,0:T(8,128)} %param.14) | copy-start | bytes 12582916
  0.6 144.3 %copy-start.1 = (f32[1,2,256,2048]{3,2,1,0:T(8,128)S(1)}, f32[1,2,256,2048]{3,2,1,0:T(8,128)}, u32[]{:S(2)}) copy-start(f32[1,2,256,2048]{3,2,1,0:T(8,128)} %param.15) | copy-start | bytes 12582916
  0.7 144.3 %copy-start.3 = (f32[1,2,64,2048]{3,2,1,0:T(8,128)S(1)}, f32[1,2,64,2048]{3,2,1,0:T(8,128)}, u32[]{:S(2)}) copy-start(f32[1,2,64,2048]{3,2,1,0:T(8,128)} %param.12) | copy-start | bytes 3145732
  145.0 1.6 %copy-start.2 = (bf16[2,256,2048]{2,1,0:T(8,128)(2,1)S(1)}, bf16[2,256,2048]{2,1,0:T(8,128)(2,1)}, u32[]{:S(2)}) copy-start(bf16[2,256,2048]{2,1,0:T(8,128)(2,1)} %get-tuple-element.11) | copy-start | bytes 6291460
  146.6 1.2 copy-start.4
  147.8 1.0 copy-start.5

commit v7 on v6

--- a/solution.py
+++ b/solution.py
@@ -16,7 +16,7 @@
 BF16 = jnp.bfloat16
 F32 = jnp.float32
 RING = 4
-VMEM_LIMIT = 54 * 1024 * 1024
+VMEM_LIMIT = 56517632
 
 
 def dot(left, right, contract=(1, 0)):
@@ -253,8 +253,8 @@
 
 def kernel(
     docs, cot_docs, route, doc_len, wt1, wt2,
-    sum1, sum2_out,
-    pick, sum2,
+    sums_out,
+    pick, sum_all,
     stage1, stage2, own1, weights1, weights2,
     normed1, act1, gate1, part1, joined1, through1, summed1, landed1, out1,
     packed, cot, rows, back,
@@ -355,7 +355,8 @@
         ]
 
     column = [down_z(m) for m in range(2)]
-    for m in (1, 0):
+
+    def cast_z(m):
         for h in range(2):
             loads[1 + 2 * m + h].wait()
             act2[h, m] = stage2[h, m].astype(BF16)
@@ -375,10 +376,6 @@
         )
         for k, buf in enumerate((cot, rows))
     ]
-    slot_matrix(route, pick)
-    live = live_rows(doc_len, lanes)
-    masked = jnp.where(live, cot_docs[:, left], jnp.zeros((lanes, half), BF16))
-    packed[...] = dot(pick[...], masked).astype(BF16).reshape(packed.shape)
 
     for m in range(2):
         for k, copy in enumerate(spread[m]):
@@ -386,12 +383,19 @@
             gathers[m][1 + k].start()
         if m == 0:
             documents.start()
-        for gather in gathers[m][:3]:
-            gather.forward()
-        if m == 1:
-            column[1][0].wait_recv()
-            column[1][2].start()
-        gathers[m][3].forward()
+            cast_z(1)
+    for gather in gathers[0][:3]:
+        gather.forward()
+    cast_z(0)
+    gathers[0][3].forward()
+    slot_matrix(route, pick)
+    live = live_rows(doc_len, lanes)
+    masked = jnp.where(live, cot_docs[:, left], jnp.zeros((lanes, half), BF16))
+    packed[...] = dot(pick[...], masked).astype(BF16).reshape(packed.shape)
+    for gather in gathers[1]:
+        gather.forward()
+    column[1][0].wait_recv()
+    column[1][2].start()
     swaps[0].start()
     documents.forward()
     documents.near()
@@ -716,16 +720,21 @@
     other_side = pl.ds(pl.multiple_of((1 - side) * hidden2, hidden2), hidden2)
     for m in (1, 0):
         sums[m][1].wait_recv()
-        sum2[m, :, own_side] = (terms2[level, m].astype(F32) + near2[m].astype(F32)).astype(BF16)
+        sum_all[m, 0:deep, own_side] = (terms2[level, m].astype(F32) + near2[m].astype(F32)).astype(BF16)
         sums[m][2].wait_recv()
-        sum2[m, :, other_side] = far2[m]
-    keep = pltpu.make_async_copy(sum2, sum2_out, local_sem.at[0])
-    keep.start()
+        sum_all[m, 0:deep, other_side] = far2[m]
+    rows2, rows1 = pl.ds(0, deep), pl.ds(deep, block)
+    keeps = [
+        pltpu.make_async_copy(sum_all.at[:, part], sums_out.at[:, part], local_sem.at[k])
+        for k, part in enumerate((rows2, rows1))
+    ]
+    keeps[0].start()
     for m in (1, 0):
         for step in (1, 3, 2):
             along_back(step, m).wait_recv()
         for q in range(RING):
-            sum1[m, :, q * hidden1:(q + 1) * hidden1] = final1[m, q]
+            sum_all[m, deep:deep + block, q * hidden1:(q + 1) * hidden1] = final1[m, q]
+    keeps[1].start()
 
     for copy in spread[0] + spread[1] + [column[0][2], column[1][2]] + sums[0] + sums[1]:
         copy.wait_send()
@@ -741,7 +750,8 @@
     to_partner(0).wait_send()
     to_partner(1).wait_send()
     swap_mean.wait_send()
-    keep.wait()
+    for keep in keeps:
+        keep.wait()
 
 
 def outer_step(scales, wt1, mom1, sum1, wt2, mom2, sum2, new_wt1, new_mom1, new_wt2, new_mom2):
@@ -753,7 +763,7 @@
 
     step(scales[1], wt2, mom2, sum2, new_wt2, new_mom2)
 
-    @pl.when(pl.program_id(0) == 0)
+    @pl.when((pl.program_id(0) == 0) & (pl.program_id(1) == 0))
     def _():
         step(scales[0], wt1, mom1, sum1, new_wt1, new_mom1)
 
@@ -779,17 +789,14 @@
         return pltpu.SemaphoreType.DMA(sizes)
 
     hold = lanes // 2
-    sum1, sum2 = pl.pallas_call(
+    sums = pl.pallas_call(
         kernel,
-        out_shape=(
-            jax.ShapeDtypeStruct((2, small, hidden), BF16),
-            jax.ShapeDtypeStruct((2, quarter, hidden), BF16),
-        ),
+        out_shape=jax.ShapeDtypeStruct((2, quarter + small, hidden), BF16),
         in_specs=[whole, whole, whole, whole, anywhere, anywhere],
-        out_specs=[whole, anywhere],
+        out_specs=anywhere,
         scratch_shapes=[
             vmem(count, lanes),
-            vmem(2, quarter, hidden),
+            vmem(2, quarter + small, hidden),
             vmem(2, small, hidden, kind=F32),
             vmem(2, 2, quarter, hidden2, kind=F32),
             vmem(RING, 2, small, hidden1),
@@ -844,29 +851,21 @@
         name="window",
     )(docs.reshape(lanes, width), cot.reshape(lanes, width), route.T, doc_len[None], wt1[0], wt2[0])
 
-    flat1, flat2 = (2 * small, hidden), (2 * quarter, hidden)
-    steps = 4
-    once = pl.BlockSpec(flat1, lambda number: (0, 0))
-    part = pl.BlockSpec((flat2[0] // steps, hidden), lambda number: (number, 0))
+    steps = 2
+    once = pl.BlockSpec((2, small, hidden), lambda m, number: (0, 0, 0))
+    part = pl.BlockSpec((1, quarter // steps, hidden), lambda m, number: (m, number, 0))
+    last = pl.BlockSpec((2, small, hidden), lambda m, number: (0, quarter // small, 0))
+    like1, like2 = (jax.ShapeDtypeStruct((2, rows, hidden), F32) for rows in (small, quarter))
     results = pl.pallas_call(
         functools.partial(outer_step, (groups, levels)),
-        grid=(steps,),
-        out_shape=[jax.ShapeDtypeStruct(flat, F32) for flat in (flat1, flat1, flat2, flat2)],
-        in_specs=[once] * 3 + [part] * 3,
-        out_specs=[once] * 2 + [part] * 2,
+        grid=(2, steps),
+        out_shape=[like1, like1, like2, like2],
+        in_specs=[once, once, last, part, part, part],
+        out_specs=[once, once, part, part],
         compiler_params=pltpu.CompilerParams(vmem_limit_bytes=24 * 1024 * 1024),
         name="outer",
-    )(
-        wt1.reshape(flat1),
-        mom1.reshape(flat1),
-        sum1.reshape(flat1),
-        wt2.reshape(flat2),
-        mom2.reshape(flat2),
-        sum2.reshape(flat2),
-    )
-    return tuple(
-        result.reshape(like.shape) for result, like in zip(results, (wt1, mom1, wt2, mom2))
-    )
+    )(wt1[0], mom1[0], sums, wt2[0], mom2[0], sums)
+    return tuple(result[None] for result in results)
 
 
 def solution(mesh):

time: 154 us -> 157 us (1.019)
  Pallas kernels: 149 us -> 153 us
    pallas_call x2, Pallas kernels: 149 us -> 153 us  [the longest x1 148 us: local(): pl.pallas_call(kernel, out_shape=jax.ShapeDtypeStruct((2, quarter + small...]
    unnamed x12 -> x14, local copies, waits for them, and re-layouts: 3.86 us -> 3.05 us
where the time goes in v7:
time: 157 us
  Pallas kernels  153 us (97%)
  local copies, waits for them, and re-layouts  3.05 us (2%)
    pallas_call x1, Pallas kernels, local(): pl.pallas_call(kernel, out_shape=jax.ShapeDtypeStruct((2, quarter + small...  148 us
    pallas_call x1, Pallas kernels, local(): pl.pallas_call(functools.partial(outer_step, (groups, levels)), grid=(2,...  5.26 us

profile of v7, /device:TPU:1, one launch (start us, length us, event | category | flops | bytes accessed | tf_op | source)
XLA Modules:
  0.0 157.0 jit_solution(12633629489961078577)
XLA Ops:
  0.6 0.0 copy-start.5
  0.6 0.6 copy-done.5
  1.3 0.0 copy-start.6
  1.3 0.7 copy-done.6
  1.9 0.0 copy-start.1
  1.9 0.0 copy-start.2
  1.9 0.0 copy-start.3
  2.0 0.0 copy-start.4
  2.0 148.0 %window.1.sum1.sum2 = bf16[2,320,2048]{2,1,0:T(8,128)(2,1)} custom-call(bf16[256,1024]{1,0:T(8,128)(2,1)} %bitcast.24, bf16[256,1024]{1,0:T(8,128)(2,1)} %bitcast.25, s32[1,16]{1,0:T(1,128)S(1)} %bitcast.18, s32[1,16]{1,0:T(1,128)S(1)} %bitcast.19, f32[2,64,2048]{2,1,0:T(8,128)} %bitcast.15, f32[2,256,2048]{2,1,0:T(8,128)} %bitcast.12), custom_call_target="tpu_custom_call" | custom-call | flops 99999997952 | bytes 40000000 | tf_op jit(solution)/shard_map/window/pallas_call | solution.py:792
  149.9 0.0 copy-done.1
  149.9 0.0 copy-done.2
  149.9 0.0 copy-done.3
  150.0 0.0 copy-done.4
  150.0 0.0 copy-start
  150.0 1.7 %copy-done = bf16[2,320,2048]{2,1,0:T(8,128)(2,1)S(1)} copy-done((bf16[2,320,2048]{2,1,0:T(8,128)(2,1)S(1)}, bf16[2,320,2048]{2,1,0:T(8,128)(2,1)}, u32[]{:S(2)}) %copy-start) | copy-done | bytes 2621464
  151.7 5.3 %outer.1 = (f32[2,64,2048]{2,1,0:T(8,128)}, f32[2,64,2048]{2,1,0:T(8,128)}, f32[2,256,2048]{2,1,0:T(8,128)}, f32[2,256,2048]{2,1,0:T(8,128)}) custom-call(f32[2,64,2048]{2,1,0:T(8,128)S(1)} %bitcast.16, f32[2,64,2048]{2,1,0:T(8,128)S(1)} %bitcast.17, bf16[2,320,2048]{2,1,0:T(8,128)(2,1)S(1)} %copy-done, f32[2,256,2048]{2,1,0:T(8,128)S(1)} %bitcast.13, ...), custom_call_target="tpu_custom_call" | custom-call | tf_op jit(solution)/shard_map/outer/pallas_call | solution.py:859
Async XLA Ops:
  0.6 0.7 copy-start.5
  1.3 0.7 copy-start.6
  1.9 148.0 %copy-start.1 = (f32[1,2,256,2048]{3,2,1,0:T(8,128)S(1)}, f32[1,2,256,2048]{3,2,1,0:T(8,128)}, u32[]{:S(2)}) copy-start(f32[1,2,256,2048]{3,2,1,0:T(8,128)} %param.14) | copy-start | bytes 12582916
  1.9 148.0 %copy-start.2 = (f32[1,2,256,2048]{3,2,1,0:T(8,128)S(1)}, f32[1,2,256,2048]{3,2,1,0:T(8,128)}, u32[]{:S(2)}) copy-start(f32[1,2,256,2048]{3,2,1,0:T(8,128)} %param.15) | copy-start | bytes 12582916
  1.9 148.0 %copy-start.3 = (f32[1,2,64,2048]{3,2,1,0:T(8,128)S(1)}, f32[1,2,64,2048]{3,2,1,0:T(8,128)}, u32[]{:S(2)}) copy-start(f32[1,2,64,2048]{3,2,1,0:T(8,128)} %param.12) | copy-start | bytes 3145732
  2.0 148.0 %copy-start.4 = (f32[1,2,64,2048]{3,2,1,0:T(8,128)S(1)}, f32[1,2,64,2048]{3,2,1,0:T(8,128)}, u32[]{:S(2)}) copy-start(f32[1,2,64,2048]{3,2,1,0:T(8,128)} %param.13) | copy-start | bytes 3145732
  150.0 1.7 %copy-start = (bf16[2,320,2048]{2,1,0:T(8,128)(2,1)S(1)}, bf16[2,320,2048]{2,1,0:T(8,128)(2,1)}, u32[]{:S(2)}) copy-start(bf16[2,320,2048]{2,1,0:T(8,128)(2,1)} %window.1.sum1.sum2) | copy-start | bytes 7864324

commit v8 on v7

--- a/solution.py
+++ b/solution.py
@@ -16,7 +16,7 @@
 BF16 = jnp.bfloat16
 F32 = jnp.float32
 RING = 4
-VMEM_LIMIT = 56517632
+VMEM_LIMIT = 54 * 1024 * 1024
 
 
 def dot(left, right, contract=(1, 0)):
@@ -355,8 +355,7 @@
         ]
 
     column = [down_z(m) for m in range(2)]
-
-    def cast_z(m):
+    for m in (1, 0):
         for h in range(2):
             loads[1 + 2 * m + h].wait()
             act2[h, m] = stage2[h, m].astype(BF16)
@@ -376,6 +375,10 @@
         )
         for k, buf in enumerate((cot, rows))
     ]
+    slot_matrix(route, pick)
+    live = live_rows(doc_len, lanes)
+    masked = jnp.where(live, cot_docs[:, left], jnp.zeros((lanes, half), BF16))
+    packed[...] = dot(pick[...], masked).astype(BF16).reshape(packed.shape)
 
     for m in range(2):
         for k, copy in enumerate(spread[m]):
@@ -383,37 +386,24 @@
             gathers[m][1 + k].start()
         if m == 0:
             documents.start()
-            cast_z(1)
-    for gather in gathers[0][:3]:
-        gather.forward()
-    cast_z(0)
-    gathers[0][3].forward()
-    slot_matrix(route, pick)
-    live = live_rows(doc_len, lanes)
-    masked = jnp.where(live, cot_docs[:, left], jnp.zeros((lanes, half), BF16))
-    packed[...] = dot(pick[...], masked).astype(BF16).reshape(packed.shape)
-    for gather in gathers[1]:
-        gather.forward()
-    column[1][0].wait_recv()
-    column[1][2].start()
+        for gather in gathers[m][:3]:
+            gather.forward()
+        if m == 1:
+            column[1][0].wait_recv()
+            column[1][2].start()
+        gathers[m][3].forward()
     swaps[0].start()
+
+    def normalize_one(pos, source):
+        floated = source.astype(F32)
+        square = jnp.sum(floated * floated, axis=-1, keepdims=True)
+        normed1[pos] = (floated * rms_of(square, width)).astype(BF16)
+
+    normalize_one(col, docs[...])
     documents.forward()
     documents.near()
     doc_pair(3).start()
     doc_pair(1).start()
-    documents.far()
-    doc_pair(2).start()
-    normed1[col] = docs[...]
-    documents.drain()
-    for step in (1, 2, 3):
-        doc_pair(step).wait()
-
-    def normalize_one(number):
-        floated = normed1[number].astype(F32)
-        square = jnp.sum(floated * floated, axis=-1, keepdims=True)
-        normed1[number] = (floated * rms_of(square, width)).astype(BF16)
-
-    each(0, RING, normalize_one)
     for gather in gathers[0]:
         gather.near()
         gather.far()
@@ -447,7 +437,15 @@
         give1(step).wait_recv()
         joined1[pos] = (part1[pos, core].astype(F32) + joined1[pos].astype(F32)).astype(BF16)
 
-    each(0, RING, up_one)
+    up_one(col)
+    documents.far()
+    doc_pair(2).start()
+    documents.drain()
+    for step in (3, 1, 2):
+        pos = wrap(col + step)
+        doc_pair(step).wait()
+        normalize_one(pos, normed1[pos])
+        up_one(pos)
     shares[0].turn()
     for gather in gathers[1]:
         gather.near()

time: 157 us -> 151 us (0.962)
  Pallas kernels: 153 us -> 147 us
    pallas_call x1, Pallas kernels: 148 us -> 142 us  [local(): pl.pallas_call(kernel, out_shape=jax.ShapeDtypeStruct((2, quarter + small...]
where the time goes in v8:
time: 151 us
  Pallas kernels  147 us (97%)
  local copies, waits for them, and re-layouts  2.97 us (2%)
    pallas_call x1, Pallas kernels, local(): pl.pallas_call(kernel, out_shape=jax.ShapeDtypeStruct((2, quarter + small...  142 us
    pallas_call x1, Pallas kernels, local(): pl.pallas_call(functools.partial(outer_step, (groups, levels)), grid=(2,...  5.12 us

profile of v8, /device:TPU:1, one launch (start us, length us, event | category | flops | bytes accessed | tf_op | source)
XLA Modules:
  0.0 151.0 jit_solution(9882434866799492272)
XLA Ops:
  0.6 0.0 copy-start.1
  0.6 0.0 copy-start.2
  0.7 0.0 copy-start.3
  0.7 142.2 %window.1.sum1.sum2 = bf16[2,320,2048]{2,1,0:T(8,128)(2,1)} custom-call(bf16[256,1024]{1,0:T(8,128)(2,1)} %bitcast.22, bf16[256,1024]{1,0:T(8,128)(2,1)} %bitcast.23, s32[1,16]{1,0:T(1,128)} %bitcast.24, s32[1,16]{1,0:T(1,128)} %bitcast.25, f32[2,64,2048]{2,1,0:T(8,128)} %bitcast.15, f32[2,256,2048]{2,1,0:T(8,128)} %bitcast.12), custom_call_target="tpu_custom_call" | custom-call | flops 99999997952 | bytes 40000000 | tf_op jit(solution)/shard_map/window/pallas_call | solution.py:790
  142.9 0.0 copy-done.1
  142.9 0.0 copy-done.2
  142.9 0.0 copy-done.3
  142.9 0.0 copy-start
  142.9 1.7 %copy-done = bf16[2,320,2048]{2,1,0:T(8,128)(2,1)S(1)} copy-done((bf16[2,320,2048]{2,1,0:T(8,128)(2,1)S(1)}, bf16[2,320,2048]{2,1,0:T(8,128)(2,1)}, u32[]{:S(2)}) %copy-start) | copy-done | bytes 2621464
  144.7 0.0 copy-start.4
  144.7 1.2 copy-done.4
  145.9 5.1 %outer.1 = (f32[2,64,2048]{2,1,0:T(8,128)}, f32[2,64,2048]{2,1,0:T(8,128)}, f32[2,256,2048]{2,1,0:T(8,128)}, f32[2,256,2048]{2,1,0:T(8,128)}) custom-call(f32[2,64,2048]{2,1,0:T(8,128)S(1)} %bitcast.16, f32[2,64,2048]{2,1,0:T(8,128)S(1)} %bitcast.17, bf16[2,320,2048]{2,1,0:T(8,128)(2,1)S(1)} %copy-done, f32[2,256,2048]{2,1,0:T(8,128)S(1)} %bitcast.13, ...), custom_call_target="tpu_custom_call" | custom-call | tf_op jit(solution)/shard_map/outer/pallas_call | solution.py:857
Async XLA Ops:
  0.6 142.3 %copy-start.1 = (f32[1,2,256,2048]{3,2,1,0:T(8,128)S(1)}, f32[1,2,256,2048]{3,2,1,0:T(8,128)}, u32[]{:S(2)}) copy-start(f32[1,2,256,2048]{3,2,1,0:T(8,128)} %param.14) | copy-start | bytes 12582916
  0.6 142.3 %copy-start.2 = (f32[1,2,256,2048]{3,2,1,0:T(8,128)S(1)}, f32[1,2,256,2048]{3,2,1,0:T(8,128)}, u32[]{:S(2)}) copy-start(f32[1,2,256,2048]{3,2,1,0:T(8,128)} %param.15) | copy-start | bytes 12582916
  0.7 142.3 %copy-start.3 = (f32[1,2,64,2048]{3,2,1,0:T(8,128)S(1)}, f32[1,2,64,2048]{3,2,1,0:T(8,128)}, u32[]{:S(2)}) copy-start(f32[1,2,64,2048]{3,2,1,0:T(8,128)} %param.12) | copy-start | bytes 3145732
  142.9 1.7 %copy-start = (bf16[2,320,2048]{2,1,0:T(8,128)(2,1)S(1)}, bf16[2,320,2048]{2,1,0:T(8,128)(2,1)}, u32[]{:S(2)}) copy-start(bf16[2,320,2048]{2,1,0:T(8,128)(2,1)} %window.1.sum1.sum2) | copy-start | bytes 7864324
  144.7 1.2 copy-start.4

commit v9 on v8

--- a/solution.py
+++ b/solution.py
@@ -139,16 +139,16 @@
 
 
 class Exchange:
-    def __init__(self, packed, land, place, send, recv):
-        self.place, self.groups = place, packed.shape[0]
+    def __init__(self, packed, land, place, send, recv, back=False):
+        self.place, self.groups, self.back = place, packed.shape[0], back
         self.packed, self.land, self.send, self.recv = packed, land, send, recv
 
     def copy(self, step):
         level, base, core = self.place
         target = lax.rem(base + step, self.groups)
         return remote(
-            self.packed.at[target],
-            self.land.at[base],
+            self.packed.at[lax.rem(self.groups - step, self.groups) if self.back else target],
+            self.land.at[base if self.back else step],
             self.send.at[step],
             self.recv.at[step],
             (level, target, core),
@@ -157,7 +157,10 @@
     def start(self):
         each(1, self.groups, lambda step: self.copy(step).start())
         base = self.place[1]
-        self.land[base] = self.packed[base]
+        if self.back:
+            self.land[base] = self.packed[0]
+        else:
+            self.land[0] = self.packed[base]
 
     def wait(self, step):
         self.copy(step).wait_recv()
@@ -172,14 +175,19 @@
         self.exchange, self.groups = exchange, exchange.groups
 
         def copy(path, step):
-            source = wrap(place[1] - step, self.groups)
-            mine = rows.at[0, core, source]
+            mine = rows.at[0, core, step]
             if path == 0:
                 return remote(mine, mine, send.at[0, step], recv.at[0, step], sibling)
-            return remote(mine, rows.at[1, core, source], send.at[1, step], recv.at[1, step], partner)
+            return remote(mine, rows.at[1, core, step], send.at[1, step], recv.at[1, step], partner)
 
         self.copy = copy
-        self.last = remote(rows.at[1, core], rows.at[1, core], last_send, last_recv, sibling)
+        self.count = self.groups // 2
+
+        def last(part):
+            where = rows.at[1, core, pl.ds(part * self.count, self.count)]
+            return remote(where, where, last_send(part), last_recv(part), sibling)
+
+        self.last = [last(part) for part in range(2)]
 
     def turn(self):
         def step(number):
@@ -196,12 +204,13 @@
     def own(self):
         each(0, self.groups, lambda step: self.copy(0, step).wait_recv())
 
-    def partner(self):
-        each(0, self.groups, lambda step: self.copy(1, step).wait_recv())
-        self.last.start()
-
-    def finish(self):
-        self.last.wait_recv()
+    def partner(self, part):
+        first = part * self.count
+        each(first, first + self.count, lambda step: self.copy(1, step).wait_recv())
+        self.last[part].start()
+
+    def finish(self, part):
+        self.last[part].wait_recv()
 
     def drain(self):
         def step(number):
@@ -209,7 +218,8 @@
             self.copy(1, number).wait_send()
 
         each(0, self.groups, step)
-        self.last.wait_send()
+        for last in self.last:
+            last.wait_send()
 
 
 def greet(devices):
@@ -365,15 +375,16 @@
 
     left = pl.ds(pl.multiple_of(core * half, half), half)
     swaps = [
-        Exchange(packed, land, place, swap_send.at[k], swap_recv.at[k])
+        Exchange(packed, land, place, swap_send.at[k], swap_recv.at[k], k == 2)
         for k, land in enumerate((cot.at[0, core], rows.at[0, core], back))
     ]
     shares = [
         Share(
             swaps[k], buf, place, partner_chip, sibling,
-            share_send.at[k], share_recv.at[k], pair_send.at[4 + k], pair_recv.at[4 + k],
-        )
-        for k, buf in enumerate((cot, rows))
+            share_send.at[k], share_recv.at[k],
+            lambda part, spots=spots: pair_send.at[spots[part]], lambda part, spots=spots: pair_recv.at[spots[part]],
+        )
+        for k, (buf, spots) in enumerate(((cot, (4, 0)), (rows, (5, 8))))
     ]
     slot_matrix(route, pick)
     live = live_rows(doc_len, lanes)
@@ -482,6 +493,8 @@
     packed[...] = dot(pick[...], out1[...]).astype(BF16).reshape(packed.shape)
     swaps[1].start()
     shares[0].own()
+    shares[0].partner(0)
+    shares[0].partner(1)
 
     def flat(ref, path, h):
         return ref[path, h].reshape(count, half)
@@ -503,21 +516,28 @@
         stage2[path, :, :, columns] = value.reshape(2, deep, tile)
 
     each(0, 2, incoming_tile)
+    shares[0].finish(0)
+    shares[0].finish(1)
+    each(2, 4, incoming_tile)
     reduce1.drain()
     for step in range(RING):
         give1(step).wait_send()
     shares[1].turn()
-    shares[0].partner()
     shares[1].own()
-
-    def normalize_two(path):
-        square = sum(
-            jnp.sum(jnp.square(flat(rows, path, h).astype(F32)), axis=-1, keepdims=True) for h in range(2)
-        )
+    shares[1].partner(0)
+
+    def normalize_two(path, first, parts):
+        each_part = groups // 2
+
+        def pieces_of(h):
+            where = slice(first * each_part, (first + parts) * each_part)
+            return rows[path, h, where].reshape(parts * deep, half).astype(F32)
+
+        square = sum(jnp.sum(jnp.square(pieces_of(h)), axis=-1, keepdims=True) for h in range(2))
         factor = rms_of(square, width)
         for h in range(2):
-            value = (flat(rows, path, h).astype(F32) * factor).astype(BF16)
-            terms1[2 * path:2 * path + 2, h] = value.reshape(2, RING, block, half)
+            value = (pieces_of(h) * factor).astype(BF16)
+            terms1[2 * path + first:2 * path + first + parts, h] = value.reshape(parts, RING, block, half)
         return factor
 
     def normed2(path, h):
@@ -540,18 +560,13 @@
 
         return step
 
-    factor = normalize_two(0)
+    factor = normalize_two(0, 0, 2)
     column[0][1].wait_recv()
     column[0][2].wait_recv()
     for m in range(2):
         column[m][0].wait_send()
         column[m][1].wait_send()
     each(0, 2, slope_tile(0, 0, 2))
-    shares[1].partner()
-    shares[0].finish()
-    each(2, 4, incoming_tile)
-    shares[1].finish()
-    normalize_two(1)
 
     def give2(spot):
         return remote(
@@ -580,10 +595,15 @@
         dn_sum[part] = dn_of(2 + part).astype(BF16)
         to_partner(part).start()
 
+    shares[1].finish(0)
+    normalize_two(1, 0, 1)
     each(0, 2, slope_tile(1, 0, 1))
     dn_tiles(1, 0, 1)
+    shares[1].partner(1)
+    dn_out(0)
+    shares[1].finish(1)
+    normalize_two(1, 1, 1)
     each(0, 2, slope_tile(1, 1, 1))
-    dn_out(0)
     dn_tiles(1, 1, 1)
     dn_out(1)
     dn_tiles(0, 0, 2)

time: 151 us -> 147 us (0.974)
  Pallas kernels: 147 us -> 144 us
    pallas_call x1, Pallas kernels: 142 us -> 139 us  [local(): pl.pallas_call(kernel, out_shape=jax.ShapeDtypeStruct((2, quarter + small...]
where the time goes in v9:
time: 147 us
  Pallas kernels  144 us (98%)
  local copies, waits for them, and re-layouts  2.97 us (2%)
    pallas_call x1, Pallas kernels, local(): pl.pallas_call(kernel, out_shape=jax.ShapeDtypeStruct((2, quarter + small...  139 us
    pallas_call x1, Pallas kernels, local(): pl.pallas_call(functools.partial(outer_step, (groups, levels)), grid=(2,...  5.12 us
    unnamed x10, local copies, waits for them, and re-layouts  2.97 us

profile of v9, /device:TPU:1, one launch (start us, length us, event | category | flops | bytes accessed | tf_op | source)
XLA Modules:
  0.0 147.3 jit_solution(16173547077897262163)
XLA Ops:
  0.6 0.0 copy-start.1
  0.6 0.0 copy-start.2
  0.7 0.0 copy-start.3
  0.7 138.5 %window.1.sum1.sum2 = bf16[2,320,2048]{2,1,0:T(8,128)(2,1)} custom-call(bf16[256,1024]{1,0:T(8,128)(2,1)} %bitcast.22, bf16[256,1024]{1,0:T(8,128)(2,1)} %bitcast.23, s32[1,16]{1,0:T(1,128)} %bitcast.24, s32[1,16]{1,0:T(1,128)} %bitcast.25, f32[2,64,2048]{2,1,0:T(8,128)} %bitcast.15, f32[2,256,2048]{2,1,0:T(8,128)} %bitcast.12), custom_call_target="tpu_custom_call" | custom-call | flops 99999997952 | bytes 40000000 | tf_op jit(solution)/shard_map/window/pallas_call | solution.py:810
  139.2 0.0 copy-done.1
  139.2 0.0 copy-done.2
  139.2 0.0 copy-done.3
  139.2 0.0 copy-start
  139.2 1.7 %copy-done = bf16[2,320,2048]{2,1,0:T(8,128)(2,1)S(1)} copy-done((bf16[2,320,2048]{2,1,0:T(8,128)(2,1)S(1)}, bf16[2,320,2048]{2,1,0:T(8,128)(2,1)}, u32[]{:S(2)}) %copy-start) | copy-done | bytes 2621464
  141.0 0.0 copy-start.4
  141.0 1.2 copy-done.4
  142.2 5.1 %outer.1 = (f32[2,64,2048]{2,1,0:T(8,128)}, f32[2,64,2048]{2,1,0:T(8,128)}, f32[2,256,2048]{2,1,0:T(8,128)}, f32[2,256,2048]{2,1,0:T(8,128)}) custom-call(f32[2,64,2048]{2,1,0:T(8,128)S(1)} %bitcast.16, f32[2,64,2048]{2,1,0:T(8,128)S(1)} %bitcast.17, bf16[2,320,2048]{2,1,0:T(8,128)(2,1)S(1)} %copy-done, f32[2,256,2048]{2,1,0:T(8,128)S(1)} %bitcast.13, ...), custom_call_target="tpu_custom_call" | custom-call | tf_op jit(solution)/shard_map/outer/pallas_call | solution.py:877
Async XLA Ops:
  0.6 138.6 %copy-start.1 = (f32[1,2,256,2048]{3,2,1,0:T(8,128)S(1)}, f32[1,2,256,2048]{3,2,1,0:T(8,128)}, u32[]{:S(2)}) copy-start(f32[1,2,256,2048]{3,2,1,0:T(8,128)} %param.14) | copy-start | bytes 12582916
  0.6 138.6 %copy-start.2 = (f32[1,2,256,2048]{3,2,1,0:T(8,128)S(1)}, f32[1,2,256,2048]{3,2,1,0:T(8,128)}, u32[]{:S(2)}) copy-start(f32[1,2,256,2048]{3,2,1,0:T(8,128)} %param.15) | copy-start | bytes 12582916
  0.7 138.6 %copy-start.3 = (f32[1,2,64,2048]{3,2,1,0:T(8,128)S(1)}, f32[1,2,64,2048]{3,2,1,0:T(8,128)}, u32[]{:S(2)}) copy-start(f32[1,2,64,2048]{3,2,1,0:T(8,128)} %param.12) | copy-start | bytes 3145732
  139.2 1.7 %copy-start = (bf16[2,320,2048]{2,1,0:T(8,128)(2,1)S(1)}, bf16[2,320,2048]{2,1,0:T(8,128)(2,1)}, u32[]{:S(2)}) copy-start(bf16[2,320,2048]{2,1,0:T(8,128)(2,1)} %window.1.sum1.sum2) | copy-start | bytes 7864324
  141.0 1.2 copy-start.4

commit v10 on v9

--- a/solution.py
+++ b/solution.py
@@ -157,10 +157,15 @@
     def start(self):
         each(1, self.groups, lambda step: self.copy(step).start())
         base = self.place[1]
-        if self.back:
-            self.land[base] = self.packed[0]
+        self.land[0] = self.packed[base]
+
+    def start_back(self, part):
+        middle = self.groups // 2
+        if part == 0:
+            each(middle + 1, self.groups, lambda step: self.copy(step).start())
+            self.land[self.place[1]] = self.packed[0]
         else:
-            self.land[0] = self.packed[base]
+            each(1, middle + 1, lambda step: self.copy(step).start())
 
     def wait(self, step):
         self.copy(step).wait_recv()
@@ -632,26 +637,27 @@
     sums[1][0].start()
     sums[1][1].start()
 
+    def swap_mean(part):
+        where = pl.ds(part * deep, deep)
+        return remote(mean_out.at[where], mean_in.at[where], col_send.at[part], col_recv.at[part], sibling)
+
+    swaps[1].drain()
     for part in range(2):
         give2(part).wait_recv()
         to_partner(part).wait_recv()
-
-    def pieces():
-        value = jnp.concatenate([dn_of(part) + dn_far[part].astype(F32) for part in range(2)], axis=0)
-        return flat(rows, 0, core).astype(F32) * factor, value
-
-    normed, value = pieces()
-    mean = jnp.sum(value * normed, axis=-1, keepdims=True)
-    mean_out[...] = jnp.broadcast_to(mean, mean_out.shape)
-    swap_mean = remote(mean_out, mean_in, pair_send.at[9], pair_recv.at[9], sibling)
-    swap_mean.start()
-    swap_mean.wait_recv()
-    mean = (mean + mean_in[:, 0:1]) / width
-    normed, value = pieces()
-    result = flat(cot, 0, core).astype(F32) + factor * (value - normed * mean)
-    swaps[1].drain()
-    packed[...] = result.astype(BF16).reshape(packed.shape)
-    swaps[2].start()
+        where = slice(part * (groups // 2), (part + 1) * (groups // 2))
+        lines = slice(part * deep, (part + 1) * deep)
+        scale = factor[lines]
+        normed = rows[0, core, where].reshape(deep, half).astype(F32) * scale
+        value = dn_of(part) + dn_far[part].astype(F32)
+        mean = jnp.sum(value * normed, axis=-1, keepdims=True)
+        mean_out[lines] = jnp.broadcast_to(mean, (deep, mean_out.shape[1]))
+        swap_mean(part).start()
+        swap_mean(part).wait_recv()
+        mean = (mean + mean_in[lines, 0:1]) / width
+        result = cot[0, core, where].reshape(deep, half).astype(F32) + scale * (value - normed * mean)
+        packed[where] = result.astype(BF16).reshape(groups // 2, -1, half)
+        swaps[2].start_back(part)
     term_tiles(0, normed2, slopes2)
     sums[0][0].start()
     sums[0][1].start()
@@ -767,7 +773,8 @@
     give2(0).wait_send()
     to_partner(0).wait_send()
     to_partner(1).wait_send()
-    swap_mean.wait_send()
+    swap_mean(0).wait_send()
+    swap_mean(1).wait_send()
     for keep in keeps:
         keep.wait()
 

time: 147 us -> 144 us (0.980)
  Pallas kernels: 144 us -> 140 us
    pallas_call x1, Pallas kernels: 139 us -> 135 us  [local(): pl.pallas_call(kernel, out_shape=jax.ShapeDtypeStruct((2, quarter + small...]
where the time goes in v10:
time: 144 us
  Pallas kernels  140 us (97%)
  local copies, waits for them, and re-layouts  2.97 us (2%)
    pallas_call x1, Pallas kernels, local(): pl.pallas_call(kernel, out_shape=jax.ShapeDtypeStruct((2, quarter + small...  135 us
    pallas_call x1, Pallas kernels, local(): pl.pallas_call(functools.partial(outer_step, (groups, levels)), grid=(2,...  5.12 us
    unnamed x10, local copies, waits for them, and re-layouts  2.97 us

profile of v10, /device:TPU:1, one launch (start us, length us, event | category | flops | bytes accessed | tf_op | source)
XLA Modules:
  0.0 143.9 jit_solution(9483516091185416123)
XLA Ops:
  0.6 0.0 copy-start.1
  0.6 0.0 copy-start.2
  0.7 0.0 copy-start.3
  0.7 135.1 %window.1.sum1.sum2 = bf16[2,320,2048]{2,1,0:T(8,128)(2,1)} custom-call(bf16[256,1024]{1,0:T(8,128)(2,1)} %bitcast.22, bf16[256,1024]{1,0:T(8,128)(2,1)} %bitcast.23, s32[1,16]{1,0:T(1,128)} %bitcast.24, s32[1,16]{1,0:T(1,128)} %bitcast.25, f32[2,64,2048]{2,1,0:T(8,128)} %bitcast.15, f32[2,256,2048]{2,1,0:T(8,128)} %bitcast.12), custom_call_target="tpu_custom_call" | custom-call | flops 99999997952 | bytes 40000000 | tf_op jit(solution)/shard_map/window/pallas_call | solution.py:817
  135.8 0.0 copy-done.1
  135.8 0.0 copy-done.2
  135.8 0.0 copy-done.3
  135.8 0.0 copy-start
  135.9 1.7 %copy-done = bf16[2,320,2048]{2,1,0:T(8,128)(2,1)S(1)} copy-done((bf16[2,320,2048]{2,1,0:T(8,128)(2,1)S(1)}, bf16[2,320,2048]{2,1,0:T(8,128)(2,1)}, u32[]{:S(2)}) %copy-start) | copy-done | bytes 2621464
  137.6 0.0 copy-start.4
  137.6 1.2 copy-done.4
  138.8 5.1 %outer.1 = (f32[2,64,2048]{2,1,0:T(8,128)}, f32[2,64,2048]{2,1,0:T(8,128)}, f32[2,256,2048]{2,1,0:T(8,128)}, f32[2,256,2048]{2,1,0:T(8,128)}) custom-call(f32[2,64,2048]{2,1,0:T(8,128)S(1)} %bitcast.16, f32[2,64,2048]{2,1,0:T(8,128)S(1)} %bitcast.17, bf16[2,320,2048]{2,1,0:T(8,128)(2,1)S(1)} %copy-done, f32[2,256,2048]{2,1,0:T(8,128)S(1)} %bitcast.13, ...), custom_call_target="tpu_custom_call" | custom-call | tf_op jit(solution)/shard_map/outer/pallas_call | solution.py:884
Async XLA Ops:
  0.6 135.2 %copy-start.1 = (f32[1,2,256,2048]{3,2,1,0:T(8,128)S(1)}, f32[1,2,256,2048]{3,2,1,0:T(8,128)}, u32[]{:S(2)}) copy-start(f32[1,2,256,2048]{3,2,1,0:T(8,128)} %param.14) | copy-start | bytes 12582916
  0.6 135.2 %copy-start.2 = (f32[1,2,256,2048]{3,2,1,0:T(8,128)S(1)}, f32[1,2,256,2048]{3,2,1,0:T(8,128)}, u32[]{:S(2)}) copy-start(f32[1,2,256,2048]{3,2,1,0:T(8,128)} %param.15) | copy-start | bytes 12582916
  0.7 135.2 %copy-start.3 = (f32[1,2,64,2048]{3,2,1,0:T(8,128)S(1)}, f32[1,2,64,2048]{3,2,1,0:T(8,128)}, u32[]{:S(2)}) copy-start(f32[1,2,64,2048]{3,2,1,0:T(8,128)} %param.12) | copy-start | bytes 3145732
  135.8 1.7 %copy-start = (bf16[2,320,2048]{2,1,0:T(8,128)(2,1)S(1)}, bf16[2,320,2048]{2,1,0:T(8,128)(2,1)}, u32[]{:S(2)}) copy-start(bf16[2,320,2048]{2,1,0:T(8,128)(2,1)} %window.1.sum1.sum2) | copy-start | bytes 7864324
  137.6 1.2 copy-start.4

commit v11 on v10

--- a/solution.py
+++ b/solution.py
@@ -693,10 +693,25 @@
         )
         joined1[pos] = (incoming * gate1[pos].astype(F32)).astype(BF16)
 
+
+    def add_term(step):
+        pos = wrap(col + step)
+        lift_pair(step).wait_recv()
+        for h in range(2):
+            value = dot(upstream[pos, h], act1[pos], (0, 0)).reshape(2, deep, hidden1)
+            if step != 0:
+                value = value + stage2[h, :, :, 0:hidden1]
+            if step == 2:
+                terms1[2 * h:2 * h + 2, 1] = value.astype(BF16).reshape(2, RING, block, hidden1)
+            else:
+                stage2[h, :, :, 0:hidden1] = value
+
+    add_term(0)
+    add_term(3)
+    add_term(1)
     lifts.far()
     lift_pair(2).start()
-    for step in range(RING):
-        lift_pair(step).wait_recv()
+    add_term(2)
 
     def term_one(m, lefts, right):
         for h in range(2):
@@ -714,7 +729,6 @@
         )
 
     plane = [scatter_x(m) for m in range(2)]
-    term_one(1, lambda h: upstream[:, h], act1)
     plane[1].start()
     each(0, RING, slope_one)
     term_one(0, lambda h: normed1[:, :, h * half:(h + 1) * half], joined1)

time: 144 us -> 144 us (level)
  no operation moved by 1% of the time
where the time goes in v11:
time: 144 us; the launch traced here: 143 us
  Pallas kernels  140 us (97%)
  local copies, waits for them, and re-layouts  2.97 us (2%)
    pallas_call x1, Pallas kernels, local(): pl.pallas_call(kernel, out_shape=jax.ShapeDtypeStruct((2, quarter + small...  135 us
    pallas_call x1, Pallas kernels, local(): pl.pallas_call(functools.partial(outer_step, (groups, levels)), grid=(2,...  5.12 us
    unnamed x10, local copies, waits for them, and re-layouts  2.97 us

profile of v11, /device:TPU:1, one launch (start us, length us, event | category | flops | bytes accessed | tf_op | source)
XLA Modules:
  0.0 143.4 jit_solution(2095273608129888249)
XLA Ops:
  0.6 0.0 copy-start.1
  0.6 0.0 copy-start.2
  0.7 0.0 copy-start.3
  0.7 134.6 %window.1.sum1.sum2 = bf16[2,320,2048]{2,1,0:T(8,128)(2,1)} custom-call(bf16[256,1024]{1,0:T(8,128)(2,1)} %bitcast.22, bf16[256,1024]{1,0:T(8,128)(2,1)} %bitcast.23, s32[1,16]{1,0:T(1,128)} %bitcast.24, s32[1,16]{1,0:T(1,128)} %bitcast.25, f32[2,64,2048]{2,1,0:T(8,128)} %bitcast.15, f32[2,256,2048]{2,1,0:T(8,128)} %bitcast.12), custom_call_target="tpu_custom_call" | custom-call | flops 99999997952 | bytes 40000000 | tf_op jit(solution)/shard_map/window/pallas_call | solution.py:831
  135.3 0.0 copy-done.1
  135.3 0.0 copy-done.2
  135.3 0.0 copy-done.3
  135.3 0.0 copy-start
  135.3 1.7 %copy-done = bf16[2,320,2048]{2,1,0:T(8,128)(2,1)S(1)} copy-done((bf16[2,320,2048]{2,1,0:T(8,128)(2,1)S(1)}, bf16[2,320,2048]{2,1,0:T(8,128)(2,1)}, u32[]{:S(2)}) %copy-start) | copy-done | bytes 2621464
  137.0 0.0 copy-start.4
  137.0 1.2 copy-done.4
  138.3 5.1 %outer.1 = (f32[2,64,2048]{2,1,0:T(8,128)}, f32[2,64,2048]{2,1,0:T(8,128)}, f32[2,256,2048]{2,1,0:T(8,128)}, f32[2,256,2048]{2,1,0:T(8,128)}) custom-call(f32[2,64,2048]{2,1,0:T(8,128)S(1)} %bitcast.16, f32[2,64,2048]{2,1,0:T(8,128)S(1)} %bitcast.17, bf16[2,320,2048]{2,1,0:T(8,128)(2,1)S(1)} %copy-done, f32[2,256,2048]{2,1,0:T(8,128)S(1)} %bitcast.13, ...), custom_call_target="tpu_custom_call" | custom-call | tf_op jit(solution)/shard_map/outer/pallas_call | solution.py:898
Async XLA Ops:
  0.6 134.6 %copy-start.1 = (f32[1,2,256,2048]{3,2,1,0:T(8,128)S(1)}, f32[1,2,256,2048]{3,2,1,0:T(8,128)}, u32[]{:S(2)}) copy-start(f32[1,2,256,2048]{3,2,1,0:T(8,128)} %param.14) | copy-start | bytes 12582916
  0.6 134.6 %copy-start.2 = (f32[1,2,256,2048]{3,2,1,0:T(8,128)S(1)}, f32[1,2,256,2048]{3,2,1,0:T(8,128)}, u32[]{:S(2)}) copy-start(f32[1,2,256,2048]{3,2,1,0:T(8,128)} %param.15) | copy-start | bytes 12582916
  0.7 134.6 %copy-start.3 = (f32[1,2,64,2048]{3,2,1,0:T(8,128)S(1)}, f32[1,2,64,2048]{3,2,1,0:T(8,128)}, u32[]{:S(2)}) copy-start(f32[1,2,64,2048]{3,2,1,0:T(8,128)} %param.12) | copy-start | bytes 3145732
  135.3 1.7 %copy-start = (bf16[2,320,2048]{2,1,0:T(8,128)(2,1)S(1)}, bf16[2,320,2048]{2,1,0:T(8,128)(2,1)}, u32[]{:S(2)}) copy-start(bf16[2,320,2048]{2,1,0:T(8,128)(2,1)} %window.1.sum1.sum2) | copy-start | bytes 7864324
  137.0 1.2 copy-start.4
